TPU v7x, 512 devices: a whole 4x8x8 slice. The times are simulated.
512 devices in a mesh: ctx: 64 (over z, y), tp: 8 (over x, core).
Axes of the slice: x: 4, y: 8, z: 8, core: 2. Of those that a mesh axis runs over, the one named last changes fastest.
Arguments:
- enc: bfloat16 [1, 1408, 24576], P(None, 'tp', 'ctx'), may hold values from -6 to 6
- w_down: bfloat16 [5, 1408, 1536], P(None, 'tp', 'ctx'), may hold values from -0.15625 to 0.15625
- w_up: bfloat16 [5, 1536, 1408], P(None, 'tp', 'ctx'), may hold values from -0.15625 to 0.15625
- cot: bfloat16 [1, 1408, 24576], P(None, 'tp', 'ctx'), may hold values from -6 to 6
Outputs:
- merged: bfloat16 [1, 1408, 24576], P(None, 'tp', 'ctx')
- grad_enc: bfloat16 [1, 1408, 24576], P(None, 'tp', 'ctx')
All inputs are finite; a program needn't handle non-finite values.
Results may differ from a plain program's by a relative error of at most 0.03.
Values may be sent and summed in bfloat16 or wider, within the bound.
A program may use at most 64 MiB of HBM per device.

v0:
```python
import jax
import jax.numpy as jnp
from jax import lax
from jax.sharding import PartitionSpec as P

root_half = 0.7071067811865476
norm_scale = 0.3989422804014327


def with_halo(cells, sides, width):
    for axis, dim in sides:
        count = lax.axis_size(axis)
        ends = count - 1
        head = lax.slice_in_dim(cells, 0, width, axis=dim)
        tail = lax.slice_in_dim(cells, cells.shape[dim] - width, cells.shape[dim], axis=dim)
        cells = jnp.concatenate(
            [
                lax.ppermute(tail, axis, [(i, (i + 1) % count) for i in range(ends)]),
                cells,
                lax.ppermute(head, axis, [((i + 1) % count, i) for i in range(ends)]),
            ],
            axis=dim,
        )
    return cells


def gelu_value(value):
    return 0.5 * value * (1.0 + jax.scipy.special.erf(value * root_half))


def gelu_slope(value):
    cumulative = 0.5 * (1.0 + jax.scipy.special.erf(value * root_half))
    return cumulative + value * jnp.exp(-0.5 * value * value) * norm_scale


def taps_sum(inputs, taps, rows):
    total = jnp.einsum(
        "bcl,co->bol", inputs[:, :, 0:rows], taps[0], preferred_element_type=jnp.float32
    )
    for offset in range(1, 5):
        total = total + jnp.einsum(
            "bcl,co->bol",
            inputs[:, :, offset : offset + rows],
            taps[offset],
            preferred_element_type=jnp.float32,
        )
    return total


def back_terms(total, padded, taps, rows):
    for offset in range(5):
        window = padded[:, :, 4 - offset : 4 - offset + rows]
        total = total + jnp.einsum(
            "bol,co->bcl", window, taps[offset], preferred_element_type=jnp.float32
        )
    return total


def shards(enc, w_down, w_up, cot):
    batch, enc_width, rows_fine = enc.shape
    rows = rows_fine // 2
    coarse_width = w_up.shape[1]
    enc_wide = enc.astype(jnp.float32)
    pooled = (enc_wide.reshape(batch, enc_width, rows, 2).sum(axis=3) * 0.5).astype(jnp.bfloat16)
    pooled_pad = with_halo(pooled, (("ctx", 2),), 2)
    down_terms = taps_sum(pooled_pad, lax.all_gather(w_down, "ctx", axis=2, tiled=True), rows)
    pre_coarse = lax.psum_scatter(
        down_terms.astype(jnp.bfloat16), "tp", scatter_dimension=1, tiled=True
    ).astype(jnp.float32)
    coarse = gelu_value(pre_coarse).astype(jnp.bfloat16)
    widened = jnp.repeat(coarse, 2, axis=2)
    widened_pad = with_halo(widened, (("ctx", 2),), 2)
    up_terms = taps_sum(widened_pad, lax.all_gather(w_up, "ctx", axis=2, tiled=True), rows_fine)
    pre_fine = lax.psum_scatter(
        up_terms.astype(jnp.bfloat16), "tp", scatter_dimension=1, tiled=True
    ).astype(jnp.float32)
    merged = (enc_wide + gelu_value(pre_fine)).astype(jnp.bfloat16)
    grad_fine = (cot.astype(jnp.float32) * gelu_slope(pre_fine)).astype(jnp.bfloat16)
    fine_all = lax.all_gather(grad_fine, "tp", axis=1, tiled=True)
    fine_pad = with_halo(fine_all, (("ctx", 2),), 2)
    fine_start = jnp.zeros((batch, coarse_width, rows_fine), jnp.float32)
    grad_widened = back_terms(
        fine_start, fine_pad, lax.all_gather(w_up, "ctx", axis=2, tiled=True), rows_fine
    )
    paired = grad_widened.reshape(batch, coarse_width, rows, 2).sum(axis=3)
    grad_coarse = (paired * gelu_slope(pre_coarse)).astype(jnp.bfloat16)
    coarse_all = lax.all_gather(grad_coarse, "tp", axis=1, tiled=True)
    coarse_pad = with_halo(coarse_all, (("ctx", 2),), 2)
    coarse_start = jnp.zeros((batch, enc_width, rows), jnp.float32)
    grad_pooled = back_terms(
        coarse_start, coarse_pad, lax.all_gather(w_down, "ctx", axis=2, tiled=True), rows
    )
    grad_enc = (cot.astype(jnp.float32) + 0.5 * jnp.repeat(grad_pooled, 2, axis=2)).astype(
        jnp.bfloat16
    )
    return (merged, grad_enc)


def solution(mesh):
    placed = (
        P(None, "tp", "ctx"),
        P(None, "tp", "ctx"),
        P(None, "tp", "ctx"),
        P(None, "tp", "ctx"),
    )
    return jax.shard_map(
        shards,
        mesh=mesh,
        in_specs=placed,
        out_specs=(P(None, "tp", "ctx"), P(None, "tp", "ctx")),
        check_vma=False,
    )
```

profile of v0, /device:TPU:1, one launch (start us, length us, event | category | flops | bytes accessed | tf_op | source)
XLA Modules:
  0.0 375.5 jit_solution(7893390348944615977)
XLA Ops:
  7.2 0.7 all-gather.4.cloned.1.call-update
  7.9 1.5 copy.28
  9.5 1.0 copy.27
  10.6 0.7 copy-done.10
  12.0 4.0 %collective-permute-start = (bf16[1,176,2]{1,2,0:T(2,128)(2,1)S(1)}, bf16[1,176,2]{1,2,0:T(2,128)(2,1)S(1)}, u32[]{:S(2)}, u32[]{:S(2)}) collective-permute-start(bf16[1,176,2]{1,2,0:T(2,128)(2,1)S(1)} %get-tuple-element.24), channel_id=1, source_target_pairs={{0,8},{8,16},{16,24},{24,32},{32,40},{40,48},{48,56},{56,64},{64,7... | collective-permute-start | bytes 2120 | tf_op jit(solution)/shard_map/ppermute | solution.py:18
  16.0 1.3 collective-permute-start.1
  17.3 82.7 %all-gather.4.cloned.1.call-done = bf16[5,176,1536]{1,2,0:T(8,128)(2,1)} async-done(((bf16[5,176,24]{1,2,0:T(8,128)(2,1)}), bf16[5,176,1536]{1,2,0:T(8,128)(2,1)}) %all-gather.4.cloned.1.call-update) | async-done | bytes 2703376 | tf_op jit(solution)/shard_map/all_gather | solution.py:66
  100.0 1.7 fusion.21
  101.7 1.6 convolution_add_fusion.6
  104.5 1.2 copy.46
  105.7 1.0 copy.60
  106.8 84.4 %all-gather.6.cloned.1.call-done = bf16[5,192,1408]{1,0,2:T(8,128)(2,1)} async-done(((bf16[5,192,22]{1,0,2:T(8,128)(2,1)}), bf16[5,192,1408]{1,0,2:T(8,128)(2,1)}) %all-gather.6.cloned.1.call-update) | async-done | bytes 2703376 | tf_op jit(solution)/shard_map/all_gather | solution.py:73
  191.2 18.0 %fusion.99 = (bf16[1,192,1408]{1,0,2:T(2,128)(2,1)S(1)}, bf16[1,192,1408]{1,0,2:T(2,128)(2,1)S(1)}, bf16[1,192,1408]{1,0,2:T(2,128)(2,1)}, bf16[1,192,1408]{1,0,2:T(2,128)(2,1)}, bf16[1,192,1408]{1,0,2:T(2,128)(2,1)}) fusion(bf16[5,192,1408]{1,0,2:T(8,128)(2,1)} %all-gather.6.cloned.1.call-done), kind=kLoop, calls=%fused_computation.148 | loop fusion | bytes 5406720 | tf_op jit(solution)/shard_map/slice | solution.py:44
  209.3 4.6 %copy.56 = bf16[1,192,1408]{2,1,0:T(8,128)(2,1)} copy(bf16[1,192,1408]{1,0,2:T(2,128)(2,1)} %get-tuple-element.14) | data formatting | bytes 1081344
  213.8 4.5 %copy.53 = bf16[1,192,1408]{2,1,0:T(8,128)(2,1)} copy(bf16[1,192,1408]{1,0,2:T(2,128)(2,1)} %get-tuple-element.12) | data formatting | bytes 1081344
  218.4 4.6 %copy.52 = bf16[1,192,1408]{2,1,0:T(8,128)(2,1)} copy(bf16[1,192,1408]{1,0,2:T(2,128)(2,1)} %get-tuple-element.13) | data formatting | bytes 1081344
  223.0 1.7 copy.54
  224.6 1.7 copy.55
  226.3 2.7 reduce-scatter.7.cloned.1.call-done
  229.1 1.0 reshape_bitcast_fusion.1
  230.6 1.3 collective-permute-start.3
  232.1 4.0 %collective-permute-start.2 = (bf16[1,192,2]{1,2,0:T(2,128)(2,1)S(1)}, bf16[1,192,2]{1,2,0:T(2,128)(2,1)S(1)}, u32[]{:S(2)}, u32[]{:S(2)}) collective-permute-start(bf16[1,192,2]{1,2,0:T(2,128)(2,1)S(1)} %get-tuple-element.21), channel_id=1, source_target_pairs={{0,8},{8,16},{16,24},{24,32},{32,40},{40,48},{48,56},{56,64},{64,7... | collective-permute-start | bytes 2312 | tf_op jit(solution)/shard_map/ppermute | solution.py:18
  238.1 0.5 convolution_add_fusion.1
  238.6 1.5 fusion.2
  240.1 6.4 %copy.48 = bf16[1,1408,384]{2,0,1:T(2,128)(2,1)S(1)} copy(bf16[1,1408,384]{1,2,0:T(8,128)(2,1)} %fusion.2) | data formatting | bytes 2162688
  246.6 1.2 copy.59
  247.8 1.1 copy.34
  248.9 37.9 %reduce-scatter.9.cloned.1.call-done = bf16[176,384]{1,0:T(8,128)(2,1)} async-done(((bf16[1408,384]{1,0:T(8,128)(2,1)}), bf16[176,384]{1,0:T(8,128)(2,1)}) %reduce-scatter.9.cloned.1.call-update) | async-done | bytes 135184
  286.8 1.0 reshape_bitcast_fusion
  288.1 0.9 fusion.47
  289.0 0.8 copy.35
  289.8 30.1 %all-gather.8.cloned.1.call-done = bf16[1,1408,384]{2,1,0:T(8,128)(2,1)} async-done(((bf16[1,176,384]{2,1,0:T(8,128)(2,1)}), bf16[1,1408,384]{2,1,0:T(8,128)(2,1)}) %all-gather.8.cloned.1.call-update) | async-done | bytes 1081360 | tf_op jit(solution)/shard_map/all_gather | solution.py:79
  319.9 1.3 fusion.100
  321.3 3.0 collective-permute-start.5
  324.2 1.5 collective-permute-start.4
  326.3 9.3 %collective-permute-done.4 = bf16[1,1408,2]{2,1,0:T(8,128)(2,1)S(1)} collective-permute-done((bf16[1,1408,2]{2,1,0:T(8,128)(2,1)S(1)}, bf16[1,1408,2]{2,1,0:T(8,128)(2,1)S(1)}, u32[]{:S(2)}, u32[]{:S(2)}) %collective-permute-start.4) | collective-permute-done | bytes 5664 | tf_op jit(solution)/shard_map/ppermute | solution.py:20
  335.7 0.6 fusion.17
  336.3 0.6 fusion.5
  337.3 0.6 fusion.14
  338.0 0.7 fusion.7
  339.9 16.0 %all_gather.17 = bf16[1,1536,192]{2,0,1:T(2,128)(2,1)S(1)} all-gather(bf16[1,192,192]{2,0,1:T(2,128)(2,1)S(1)} %copy.37), channel_id=1, replica_groups=mesh['ctx'=64,'tp'=8] {'tp'}, dimensions={1}, use_global_device_ids=true | all-gather | bytes 663552 | tf_op jit(solution)/shard_map/all_gather | solution.py:87
  355.9 0.9 copy.39
  356.8 1.3 collective-permute-start.6
  358.1 0.8 copy.44
  358.9 4.0 %collective-permute-start.7 = (bf16[1,1536,2]{1,2,0:T(2,128)(2,1)S(1)}, bf16[1,1536,2]{1,2,0:T(2,128)(2,1)S(1)}, u32[]{:S(2)}, u32[]{:S(2)}) collective-permute-start(bf16[1,1536,2]{1,2,0:T(2,128)(2,1)S(1)} %get-tuple-element.17), channel_id=1, source_target_pairs={{0,8},{8,16},{16,24},{24,32},{32,40},{40,48},{48,56},{56,64},{64,7... | collective-permute-start | bytes 18440 | tf_op jit(solution)/shard_map/ppermute | solution.py:18
  362.9 1.7 fusion.20
  364.6 1.6 convolution_add_fusion.12
  368.1 0.8 copy.45
  (80 shorter events, 9.3 us)
Async XLA Ops:
  7.2 92.8 %all-gather.4.cloned.1.call-start = ((), (), s32[]{:S(2)}) async-start(), calls=%async_computation.2 | async-start | bytes 3993600 | tf_op jit(solution)/shard_map/all_gather | solution.py:66
  7.9 183.3 %all-gather.6.cloned.1.call-start = ((), (), s32[]{:S(2)}) async-start(), calls=%async_computation.3 | async-start | bytes 5857280 | tf_op jit(solution)/shard_map/all_gather | solution.py:73
  9.5 219.6 %reduce-scatter.7.cloned.1.call-start = ((), (), s32[]{:S(2)}) async-start(), calls=%async_computation.5 | async-start | bytes 884736
  10.5 0.7 copy-start.10
  12.0 5.3 %collective-permute-start = (bf16[1,176,2]{1,2,0:T(2,128)(2,1)S(1)}, bf16[1,176,2]{1,2,0:T(2,128)(2,1)S(1)}, u32[]{:S(2)}, u32[]{:S(2)}) collective-permute-start(bf16[1,176,2]{1,2,0:T(2,128)(2,1)S(1)} %get-tuple-element.24), channel_id=1, source_target_pairs={{0,8},{8,16},{16,24},{24,32},{32,40},{40,48},{48,56},{56,64},{64,7... | collective-permute-start | bytes 2120 | tf_op jit(solution)/shard_map/ppermute | solution.py:18
  16.0 87.7 %collective-permute-start.1 = (bf16[1,176,2]{1,2,0:T(2,128)(2,1)S(1)}, bf16[1,176,2]{1,2,0:T(2,128)(2,1)S(1)}, u32[]{:S(2)}, u32[]{:S(2)}) collective-permute-start(bf16[1,176,2]{1,2,0:T(2,128)(2,1)S(1)} %get-tuple-element.23), channel_id=1, source_target_pairs={{8,0},{16,8},{24,16},{32,24},{40,32},{48,40},{56,48},{64,56},{72,6... | collective-permute-start | bytes 2120 | tf_op jit(solution)/shard_map/ppermute | solution.py:20
  100.0 3.3 copy-start.1
  106.8 180.0 %reduce-scatter.9.cloned.1.call-start = ((), (), s32[]{:S(2)}) async-start(), calls=%async_computation.6 | async-start | bytes 1216512
  226.3 12.3 %copy-start.4 = (bf16[1,192,1408]{2,1,0:T(8,128)(2,1)}, bf16[1,192,1408]{2,1,0:T(8,128)(2,1)S(1)}, u32[]{:S(2)}) copy-start(bf16[1,192,1408]{2,1,0:T(8,128)(2,1)S(1)} %copy.55) | copy-start | bytes 1622020
  226.3 9.8 %copy-start.6 = (bf16[1,192,1408]{2,1,0:T(8,128)(2,1)S(1)}, bf16[1,192,1408]{2,1,0:T(8,128)(2,1)}, u32[]{:S(2)}) copy-start(bf16[1,192,1408]{2,1,0:T(8,128)(2,1)} %copy.56) | copy-start | bytes 1622020
  230.6 5.5 %collective-permute-start.3 = (bf16[1,192,2]{1,2,0:T(2,128)(2,1)S(1)}, bf16[1,192,2]{1,2,0:T(2,128)(2,1)S(1)}, u32[]{:S(2)}, u32[]{:S(2)}) collective-permute-start(bf16[1,192,2]{1,2,0:T(2,128)(2,1)S(1)} %get-tuple-element.22), channel_id=1, source_target_pairs={{8,0},{16,8},{24,16},{32,24},{40,32},{48,40},{56,48},{64,56},{72,6... | collective-permute-start | bytes 2312 | tf_op jit(solution)/shard_map/ppermute | solution.py:20
  232.1 4.7 %collective-permute-start.2 = (bf16[1,192,2]{1,2,0:T(2,128)(2,1)S(1)}, bf16[1,192,2]{1,2,0:T(2,128)(2,1)S(1)}, u32[]{:S(2)}, u32[]{:S(2)}) collective-permute-start(bf16[1,192,2]{1,2,0:T(2,128)(2,1)S(1)} %get-tuple-element.21), channel_id=1, source_target_pairs={{0,8},{8,16},{16,24},{24,32},{32,40},{40,48},{48,56},{56,64},{64,7... | collective-permute-start | bytes 2312 | tf_op jit(solution)/shard_map/ppermute | solution.py:18
  236.1 1.0 copy-start.8
  236.6 1.1 copy-start.3
  247.8 40.3 %copy-start.11 = (bf16[1,176,384]{1,2,0:T(8,128)(2,1)S(1)}, bf16[1,176,384]{1,2,0:T(8,128)(2,1)}, u32[]{:S(2)}) copy-start(bf16[1,176,384]{1,2,0:T(8,128)(2,1)} %copy-done.10) | copy-start | bytes 405508
  247.8 72.1 %all-gather.8.cloned.1.call-start = ((), (), s32[]{:S(2)}) async-start(), calls=%async_computation.4 | async-start | bytes 1216512 | tf_op jit(solution)/shard_map/all_gather | solution.py:79
  248.9 72.3 %copy-start.12 = (bf16[1,176,384]{1,2,0:T(8,128)(2,1)}, bf16[1,176,384]{1,2,0:T(8,128)(2,1)S(1)}, u32[]{:S(2)}) copy-start(bf16[1,176,384]{1,2,0:T(8,128)(2,1)S(1)} %copy.34) | copy-start | bytes 405508
  319.9 5.8 %copy-start = (bf16[1,1408,384]{2,1,0:T(8,128)(2,1)S(1)}, bf16[1,1408,384]{2,1,0:T(8,128)(2,1)}, u32[]{:S(2)}) copy-start(bf16[1,1408,384]{2,1,0:T(8,128)(2,1)} %all-gather.8.cloned.1.call-done) | copy-start | bytes 3244036
  321.3 15.6 %collective-permute-start.5 = (bf16[1,1408,2]{2,1,0:T(8,128)(2,1)S(1)}, bf16[1,1408,2]{2,1,0:T(8,128)(2,1)S(1)}, u32[]{:S(2)}, u32[]{:S(2)}) collective-permute-start(bf16[1,1408,2]{2,1,0:T(8,128)(2,1)S(1)} %get-tuple-element.16), channel_id=1, source_target_pairs={{0,8},{8,16},{16,24},{24,32},{32,40},{40,48},{48,56},{56,64},{64,7... | collective-permute-start | bytes 16904 | tf_op jit(solution)/shard_map/ppermute | solution.py:18
  324.2 11.3 %collective-permute-start.4 = (bf16[1,1408,2]{2,1,0:T(8,128)(2,1)S(1)}, bf16[1,1408,2]{2,1,0:T(8,128)(2,1)S(1)}, u32[]{:S(2)}, u32[]{:S(2)}) collective-permute-start(bf16[1,1408,2]{2,1,0:T(8,128)(2,1)S(1)} %get-tuple-element.15), channel_id=1, source_target_pairs={{8,0},{16,8},{24,16},{32,24},{40,32},{48,40},{56,48},{64,56},{72,6... | collective-permute-start | bytes 16904 | tf_op jit(solution)/shard_map/ppermute | solution.py:20
  326.2 9.5 %copy-start.9 = (bf16[1,192,1408]{2,1,0:T(8,128)(2,1)S(1)}, bf16[1,192,1408]{2,1,0:T(8,128)(2,1)}, u32[]{:S(2)}) copy-start(bf16[1,192,1408]{2,1,0:T(8,128)(2,1)} %copy.53) | copy-start | bytes 1622020
  336.3 1.0 copy-start.7
  336.9 1.1 copy-start.5
  355.9 2.3 copy-start.14
  356.8 6.1 %collective-permute-start.6 = (bf16[1,1536,2]{1,2,0:T(2,128)(2,1)S(1)}, bf16[1,1536,2]{1,2,0:T(2,128)(2,1)S(1)}, u32[]{:S(2)}, u32[]{:S(2)}) collective-permute-start(bf16[1,1536,2]{1,2,0:T(2,128)(2,1)S(1)} %get-tuple-element.18), channel_id=1, source_target_pairs={{8,0},{16,8},{24,16},{32,24},{40,32},{48,40},{56,48},{64,56},{72,6... | collective-permute-start | bytes 18440 | tf_op jit(solution)/shard_map/ppermute | solution.py:20
  358.9 7.7 %collective-permute-start.7 = (bf16[1,1536,2]{1,2,0:T(2,128)(2,1)S(1)}, bf16[1,1536,2]{1,2,0:T(2,128)(2,1)S(1)}, u32[]{:S(2)}, u32[]{:S(2)}) collective-permute-start(bf16[1,1536,2]{1,2,0:T(2,128)(2,1)S(1)} %get-tuple-element.17), channel_id=1, source_target_pairs={{0,8},{8,16},{16,24},{24,32},{32,40},{40,48},{48,56},{56,64},{64,7... | collective-permute-start | bytes 18440 | tf_op jit(solution)/shard_map/ppermute | solution.py:18
  362.9 3.3 copy-start.2
  367.1 1.0 copy-start.13
Sparse Core Ops, SparseCore 0:
  11.1 88.8 all-gather.3
  103.5 87.6 all-gather.5
  194.1 34.9 reduce-scatter.6
  247.9 38.8 reduce-scatter.8
  289.9 29.9 all-gather.7
where the time goes:
time: 381 us; the launch traced here: 375 us
  waiting for transfers between devices  248 us (65%)
  local copies, waits for them, and re-layouts  59.1 us (16%)
  starting transfers between devices  20.5 us (5%)
  blocking collectives  16 us (4%)
  matrix products  15.4 us (4%)
  between operations  14.4 us (4%)
    all_gather x1, waiting for transfers between devices, shards(): lax.all_gather(w_up, 'ctx', axis=2, tiled=True)  84.4 us
    all_gather x1, waiting for transfers between devices, shards(): lax.all_gather(w_down, 'ctx', axis=2, tiled=True)  82.7 us
    unnamed x7, waiting for transfers between devices  41.4 us
    unnamed x50, local copies, waits for them, and re-layouts  36.1 us
    all_gather x1, waiting for transfers between devices, shards(): fine_all = lax.all_gather(grad_fine, 'tp', axis=1, tiled=True)  30.1 us
    slice x1, local copies, waits for them, and re-layouts, taps_sum(): taps[offset]  18 us
    all_gather x1, blocking collectives, shards(): coarse_all = lax.all_gather(grad_coarse, 'tp', axis=1, tiled=True)  16 us
    ppermute x4, starting transfers between devices, with_halo(): lax.ppermute(tail, axis, [(i, (i + 1) % count) for i in range(ends)])  14.9 us
  transfers between devices with their start and end apart: 13, of which 7 were waited for; matrix products, arithmetic and copies ran while one was open for 14% of the time, Pallas kernels for 0%

commit v1 on v0

v1 whole, which is shorter than its diff:
```python
import jax
import jax.numpy as jnp
from jax import lax
from jax.experimental import pallas as pl
from jax.experimental.pallas import tpu as pltpu
from jax.sharding import PartitionSpec as P

MESH = pl.DeviceIdType.MESH
bf16 = jnp.bfloat16
f32 = jnp.float32
root_half = 0.7071067811865476
norm_scale = 0.3989422804014327

RING = 8
GROUPS = 8
FINE_C, COARSE_C = 176, 192
OUT1, OUT2 = 24, 22
ROWS = 24
L1, L2 = 896, 1024
POS, LANES, EDGE = 192, 256, 32
FINE = 384
WIDE = 128 + FINE + 128


def erf(value):
    return lax.erf(value)


def gelu_value(value):
    return 0.5 * value * (1.0 + erf(value * root_half))


def gelu_both(value):
    cumulative = 0.5 * (1.0 + erf(value * root_half))
    return value * cumulative, cumulative + value * jnp.exp(-0.5 * value * value) * norm_scale


def gelu_slope(value):
    return gelu_both(value)[1]


def dot(a, b):
    return jnp.dot(a, b, preferred_element_type=f32)


def dot_first(a, b):
    return lax.dot_general(a, b, (((0,), (0,)), ((), ())), preferred_element_type=f32)


def iota(shape, dim):
    return lax.broadcasted_iota(jnp.int32, shape, dim)


def flat(block):
    lanes = block.shape[-1]
    return block.astype(f32).reshape(RING * ROWS, lanes).astype(bf16)


def transposed(value, width):
    if width < LANES:
        value = jnp.concatenate([value, jnp.zeros((LANES, LANES - width), f32)], axis=1)
    return jnp.transpose(value)[:width]


def shift(value, amount, axis):
    size = value.shape[axis]
    return value if amount % size == 0 else pltpu.roll(value, amount % size, axis=axis)


def kernel(
    enc_ref, cot_ref, w1_ref, w2_ref, merged_ref, genc_ref,
    enc_wide, cot_wide, w1_all, w1_swap, w1_use, w2_all, w2_swap, w2_use,
    pooled_own, pooled_other, x1, p1_send, p1_recv, pre_c, c_own, c_other, x2,
    enc_rows, cot_rows, merged_rows, p2_send, p2_recv, g_send, g_recv, y1, y2, gc_out, gc_in,
    gc_send, gc_recv, y4, gp_out, gp_in,
    halo_s, halo_r, first_s, first_r, second_s, second_r, last_s, last_r, swap_s, swap_r,
    pair_s, pair_r, tp_s, tp_r,
):
    ctx, t = lax.axis_index("ctx"), lax.axis_index("tp")
    core = lax.rem(t, 2)
    mate = t + 1 - 2 * core
    z, y = lax.div(ctx, RING), lax.rem(ctx, RING)
    one = z + (y - z) * core
    two = y + (z - y) * core

    def ring(index, step):
        return lax.rem(index + RING + step, RING)

    def place(i, j):
        straight, crossed = i * RING + j, j * RING + i
        return straight + (crossed - straight) * core

    def remote(src, dst, send, recv, device):
        return pltpu.make_async_remote_copy(
            src_ref=src, dst_ref=dst, send_sem=send, recv_sem=recv, device_id=device, device_id_type=MESH
        )

    first_to = ((place(ring(one, 1), two), t), (place(ring(one, -1), two), t))
    second_to = ((place(one, ring(two, 1)), t), (place(one, ring(two, -1)), t))
    count = RING * RING
    ctx_next, ctx_prev = lax.rem(ctx + 1, count), lax.rem(ctx + count - 1, count)

    barrier = pltpu.get_barrier_semaphore()
    partners = [*first_to, *second_to, (ctx_next, t), (ctx_prev, t)]
    partners += [(ctx, lax.rem(t + d, GROUPS)) for d in range(1, GROUPS)]
    for device in partners:
        pl.semaphore_signal(barrier, inc=1, device_id=device, device_id_type=MESH)

    taps = ((w1_ref, w1_all, w1_swap), (w2_ref, w2_all, w2_swap))
    for w_ref, w_all, _ in taps:
        w_all[two, lax.div(one, 2), lax.rem(one, 2)] = w_ref[...]
    enc_wide[:, 128 : 128 + FINE] = enc_ref[...]
    cot_wide[:, 128 : 128 + FINE] = cot_ref[...]
    pl.semaphore_wait(barrier, len(partners))

    def halo(n, side):
        source, wide = ((enc_ref, enc_wide), (cot_ref, cot_wide))[n]
        if side == 0:
            src, dst, to = source.at[:, FINE - 128 : FINE], wide.at[:, 0:128], ctx_next
        else:
            src, dst, to = source.at[:, 0:128], wide.at[:, 128 + FINE : WIDE], ctx_prev
        return remote(src, dst, halo_s.at[n, side], halo_r.at[n, side], (to, t))

    def first(w, side, hop, arriving=False):
        step = hop if arriving else hop - 1
        index = ring(one, -step if side == 0 else step)
        block = taps[w][1].at[two, lax.div(index, 2), lax.rem(index, 2)]
        return remote(block, block, first_s.at[w, side, hop], first_r.at[w, side, hop], first_to[side])

    def second(w, side, hop, half, arriving=False):
        step = hop if arriving else hop - 1
        index = ring(two, -step if side == 0 else step)
        block = taps[w][1].at[index, pl.ds(2 * half, 2)]
        return remote(
            block, block, second_s.at[w, side, hop, half], second_r.at[w, side, hop, half], second_to[side]
        )

    def swap_zero(w, index):
        return remote(
            taps[w][1].at[index], taps[w][2].at[lax.div(index, 2)],
            swap_s.at[w, lax.div(index, 2)], swap_r.at[w, lax.div(index, 2)], (ctx, mate),
        )

    def swap_one(w, index):
        return remote(
            taps[w][1].at[index, :, 0], taps[w][2].at[:, lax.div(index, 2), lax.rem(index, 2)],
            swap_s.at[w, index], swap_r.at[w, index], (ctx, mate),
        )

    def swap(w, index):
        @pl.when(jnp.logical_and(core == 0, lax.rem(index, 2) == 1))
        def _():
            swap_zero(w, index).start()

        @pl.when(core == 1)
        def _():
            swap_one(w, index).start()

    def swap_done(w):
        @pl.when(core == 0)
        def _():
            for index in range(RING):
                swap_one(w, index).wait_recv()

        @pl.when(core == 1)
        def _():
            for index in range(1, RING, 2):
                swap_zero(w, index).wait_recv()

    def swap_sent(w):
        @pl.when(core == 0)
        def _():
            for index in range(1, RING, 2):
                swap_zero(w, index).wait_send()

        @pl.when(core == 1)
        def _():
            for index in range(RING):
                swap_one(w, index).wait_send()

    hops_first = {0: 4, 1: 3}

    def first_start(w, hop):
        for side in (0, 1):
            if hop <= hops_first[side]:
                first(w, side, hop).start()

    def first_step(w, hop):
        for side in (0, 1):
            if hop <= hops_first[side]:
                first(w, side, hop, True).wait_recv()
                if hop < hops_first[side]:
                    first(w, side, hop + 1).start()

    def second_start(w):
        for half in (0, 1):
            for side in (0, 1):
                second(w, side, 1, half).start()
        swap(w, two)

    def second_step(w, hop):
        if hop < 4:
            for half in (0, 1):
                for side in (0, 1):
                    second(w, side, hop, half, True).wait_recv()
                    if hop < 3 or half == side:
                        second(w, side, hop + 1, half).start()
            swap(w, ring(two, hop))
            swap(w, ring(two, -hop))
        else:
            for side in (0, 1):
                second(w, side, 4, side, True).wait_recv()
            swap(w, ring(two, 4))

    def pair(n, src, dst):
        return remote(src, dst, pair_s.at[n], pair_r.at[n], (ctx, mate))

    def to_group(n, d, src, dst):
        return remote(src, dst, tp_s.at[n, d], tp_r.at[n, d], (ctx, lax.rem(t + d, GROUPS)))

    def scatter(n, send, recv, d):
        return to_group(n, d, send.at[lax.rem(t + d, GROUPS)], recv.at[t])

    def gather(n, send, recv, d):
        return to_group(n, d, send.at[lax.rem(lax.rem(t + d, GROUPS), 2)], recv.at[t])

    order = (4, 3, 5, 2, 6, 1, 7)

    def pack_taps(w, q):
        w_all, w_swap, use, lanes = ((w1_all, w1_swap, w1_use, L1), (w2_all, w2_swap, w2_use, L2))[w]

        def put(block, other):
            if w == 0:
                use[q, :, other * L1 : (other + 1) * L1] = flat(block)
            else:
                use[q, :, other * 640 : (other + 1) * 640] = flat(block[..., 0:640])
                use[q, :, 1280 + other * 384 : 1280 + (other + 1) * 384] = flat(block[..., 640:1024])

        @pl.when(core == 0)
        def _():
            put(w_all[2 * q], 0)

        @pl.when(core == 1)
        def _():
            put(w_all[:, q, 1], 0)

        put(w_swap[q], 1)

    for n in (0, 1):
        for side in (0, 1):
            halo(n, side).start()
    first_start(0, 1)

    for hop in (1, 2, 3, 4):
        first_step(0, hop)
    second_start(0)
    first_start(1, 1)

    for n in (0, 1):
        for side in (0, 1):
            halo(n, side).wait_recv()
    lane = iota((WIDE, 2 * LANES), 1)
    row = iota((WIDE, 2 * LANES), 0)
    half_lane = lax.rem(lane, LANES)
    pick = jnp.where(row == 2 * half_lane + 64 + lax.div(lane, LANES), 1.0, 0.0).astype(bf16)
    where_to = iota((RING * ROWS, FINE_C), 1)
    spread = jnp.where(
        iota((RING * ROWS, FINE_C), 0) == lax.div(where_to, OUT2) * ROWS + lax.rem(where_to, OUT2), 1.0, 0.0
    ).astype(bf16)
    at = ctx * POS + iota((1, LANES), 1) - EDGE
    inside = jnp.logical_and(at >= 0, at < count * POS)
    enc_ed = dot(enc_wide[...], pick)
    pooled = jnp.where(inside, (enc_ed[:, 0:LANES] + enc_ed[:, LANES:]) * 0.5, 0.0)
    pooled_own[...] = pooled.astype(bf16)
    pair(0, pooled_own, pooled_other).start()
    first_step(1, 1)
    enc_rows[...] = dot(spread, enc_ed.astype(bf16)).reshape(RING, ROWS, 2 * LANES).astype(bf16)
    cot_ed = dot(cot_wide[...], pick).astype(bf16)
    cot_rows[...] = dot(spread, cot_ed).reshape(RING, ROWS, 2 * LANES).astype(bf16)
    first_step(1, 2)
    pair(0, pooled_own, pooled_other).wait_recv()
    for other, ref in enumerate((pooled_own, pooled_other)):
        value = ref[...].astype(f32)
        for k in range(5):
            start = other * L1 + k * FINE_C
            x1[start : start + FINE_C] = shift(value, 2 - k, 1).astype(bf16)
        x1[other * L1 + 880 : (other + 1) * L1] = jnp.zeros((16, LANES), bf16)
    first_step(1, 3)
    first_step(1, 4)
    second_step(0, 1)
    second_step(0, 2)
    second_step(0, 3)
    second_start(1)
    second_step(0, 4)
    swap_done(0)

    @pl.loop(0, 4)
    def _(q):
        pack_taps(0, q)
        part = dot(w1_use[q], x1[...])
        p1_send[:, q] = part.reshape(RING, ROWS, LANES).astype(bf16)

    for d in order:
        scatter(0, p1_send, p1_recv, d).start()
    p1_recv[t] = p1_send[t]
    second_step(1, 1)
    for d in order:
        scatter(0, p1_send, p1_recv, d).wait_recv()
    sides = [sum(p1_recv[2 * x + p].astype(f32) for x in range(4)) for p in (0, 1)]
    pre_c[...] = jnp.stack(sides, axis=1).reshape(COARSE_C, LANES)
    c_own[...] = jnp.where(inside, gelu_value(pre_c[...]), 0.0).astype(bf16)
    pair(1, c_own, c_other).start()
    second_step(1, 2)
    pair(1, c_own, c_other).wait_recv()
    for other, ref in enumerate((c_own, c_other)):
        value = ref[...]
        wide = value.astype(f32)
        before, after = shift(wide, 1, 1).astype(bf16), shift(wide, -1, 1).astype(bf16)
        for start, even, odd in (
            (other * 640, before, before),
            (other * 640 + 192, value, value),
            (other * 640 + 384, after, after),
            (1280 + other * 384, before, value),
            (1280 + other * 384 + 192, value, after),
        ):
            x2[start : start + COARSE_C, 0:LANES] = even
            x2[start : start + COARSE_C, LANES : 2 * LANES] = odd
        x2[other * 640 + 576 : (other + 1) * 640] = jnp.zeros((64, 2 * LANES), bf16)
    second_step(1, 3)
    second_step(1, 4)
    swap_done(1)

    @pl.loop(0, 4)
    def _(q):
        pack_taps(1, q)
        part = dot(w2_use[q], x2[...])
        p2_send[:, q] = part.reshape(RING, ROWS, 2 * LANES).astype(bf16)

    for d in order:
        scatter(1, p2_send, p2_recv, d).start()
    p2_recv[t] = p2_send[t]
    for d in order:
        scatter(1, p2_send, p2_recv, d).wait_recv()

    @pl.loop(0, 4)
    def _(q):
        for p in (0, 1):
            pre = sum(p2_recv[2 * x + p, q].astype(f32) for x in range(4))
            value, slope = gelu_both(pre)
            merged_rows[2 * q + p] = (enc_rows[2 * q + p].astype(f32) + value).astype(bf16)
            grad = (cot_rows[2 * q + p].astype(f32) * slope).astype(bf16).astype(f32)
            even = jnp.where(inside, grad[:, 0:LANES], 0.0)
            odd = jnp.where(inside, grad[:, LANES:], 0.0)
            g_send[p, q, :, 0:LANES] = (even + odd).astype(bf16)
            g_send[p, q, :, LANES : 2 * LANES] = (even + shift(odd, 1, 1)).astype(bf16)

    for d in order:
        gather(2, g_send, g_recv, d).start()
    g_recv[t] = g_send[core]

    back = iota((2 * LANES, FINE), 1)
    unpick = jnp.where(
        iota((2 * LANES, FINE), 0) == lax.rem(back, 2) * LANES + lax.div(back, 2) + EDGE, 1.0, 0.0
    ).astype(bf16)
    kept = dot_first(spread, flat(merged_rows[...])).astype(bf16)
    merged_ref[...] = dot(kept, unpick).astype(bf16)

    for d in order:
        gather(2, g_send, g_recv, d).wait_recv()
    y1[...] = jnp.zeros_like(y1)
    y2[...] = jnp.zeros_like(y2)

    @pl.loop(0, 4)
    def _(q):
        block = flat(g_recv[:, q])
        y1[...] += dot_first(block[:, 0:LANES], w2_use[q, :, 0:1280])
        y2[...] += dot_first(block[:, LANES:], w2_use[q, :, 1280:2048])

    def coarse_part(other):
        a, b = other * 640, other * 384
        total = shift(y1[:, a : a + 192] + y2[:, b : b + 192], -1, 0)
        total = total + y1[:, a + 192 : a + 384] + y2[:, b + 192 : b + 384]
        total = total + shift(y1[:, a + 384 : a + 576], 1, 0)
        return transposed(total, COARSE_C)

    gc_out[...] = coarse_part(1)
    pair(2, gc_out, gc_in).start()
    own = coarse_part(0)
    slope = gelu_slope(pre_c[...])
    pair(2, gc_out, gc_in).wait_recv()
    grad_c = jnp.where(inside, (own + gc_in[...]) * slope, 0.0).reshape(4, 2, ROWS, LANES).astype(bf16)
    gc_send[0] = grad_c[:, 0]
    gc_send[1] = grad_c[:, 1]
    for d in order:
        gather(3, gc_send, gc_recv, d).start()
    gc_recv[t] = gc_send[core]
    y4[...] = jnp.zeros_like(y4)
    for d in order:
        gather(3, gc_send, gc_recv, d).wait_recv()

    @pl.loop(0, 4)
    def _(q):
        y4[...] += dot_first(flat(gc_recv[:, q]), w1_use[q])

    def fine_part(other):
        total = None
        for k in range(5):
            start = other * L1 + k * FINE_C
            term = shift(y4[:, start : start + FINE_C], k - 2, 0)
            total = term if total is None else total + term
        return transposed(total, FINE_C)

    gp_out[...] = fine_part(1)
    pair(3, gp_out, gp_in).start()
    own = fine_part(0)
    coarse_row = iota((LANES, FINE), 0)
    widen = jnp.where(coarse_row == lax.div(iota((LANES, FINE), 1), 2) + EDGE, 1.0, 0.0).astype(bf16)
    pair(3, gp_out, gp_in).wait_recv()
    total = (own + gp_in[...]) * 0.5
    high = total.astype(bf16)
    low = (total - high.astype(f32)).astype(bf16)
    genc_ref[...] = (cot_ref[...].astype(f32) + dot(high, widen) + dot(low, widen)).astype(bf16)

    for n in (0, 1):
        for side in (0, 1):
            halo(n, side).wait_send()
    for w in (0, 1):
        for side in (0, 1):
            for hop in range(1, hops_first[side] + 1):
                first(w, side, hop).wait_send()
            for hop in (1, 2, 3):
                for half in (0, 1):
                    second(w, side, hop, half).wait_send()
            second(w, side, 4, side).wait_send()
        swap_sent(w)
    pair(0, pooled_own, pooled_other).wait_send()
    pair(1, c_own, c_other).wait_send()
    pair(2, gc_out, gc_in).wait_send()
    pair(3, gp_out, gp_in).wait_send()
    for d in order:
        scatter(0, p1_send, p1_recv, d).wait_send()
        scatter(1, p2_send, p2_recv, d).wait_send()
        gather(2, g_send, g_recv, d).wait_send()
        gather(3, gc_send, gc_recv, d).wait_send()


def shards(enc, w_down, w_up, cot):
    w1 = jnp.transpose(w_down, (2, 0, 1)).reshape(OUT1, 5 * FINE_C)
    w1 = jnp.pad(w1, ((0, 0), (0, L1 - 5 * FINE_C)))
    up = jnp.transpose(w_up, (2, 0, 1))
    even = up[:, 0::2].reshape(OUT2, 3 * COARSE_C)
    odd = up[:, 1::2].reshape(OUT2, 2 * COARSE_C)
    w2 = jnp.concatenate([jnp.pad(even, ((0, 0), (0, 64))), odd], axis=1)
    w2 = jnp.pad(w2, ((0, ROWS - OUT2), (0, 0)))
    dma = pltpu.SemaphoreType.DMA
    vmem = pltpu.VMEM
    merged, grad_enc = pl.pallas_call(
        kernel,
        out_shape=[jax.ShapeDtypeStruct((FINE_C, FINE), bf16)] * 2,
        in_specs=[pl.BlockSpec(memory_space=vmem)] * 4,
        out_specs=[pl.BlockSpec(memory_space=vmem)] * 2,
        scratch_shapes=[
            vmem((FINE_C, WIDE), bf16),
            vmem((FINE_C, WIDE), bf16),
            vmem((RING, 4, 2, ROWS, L1), bf16),
            vmem((4, 4, 2, ROWS, L1), bf16),
            vmem((4, RING * ROWS, 2 * L1), bf16),
            vmem((RING, 4, 2, ROWS, L2), bf16),
            vmem((4, 4, 2, ROWS, L2), bf16),
            vmem((4, RING * ROWS, 2 * L2), bf16),
            vmem((FINE_C, LANES), bf16),
            vmem((FINE_C, LANES), bf16),
            vmem((2 * L1, LANES), bf16),
            vmem((GROUPS, 4, ROWS, LANES), bf16),
            vmem((GROUPS, 4, ROWS, LANES), bf16),
            vmem((COARSE_C, LANES), f32),
            vmem((COARSE_C, LANES), bf16),
            vmem((COARSE_C, LANES), bf16),
            vmem((2 * L2, 2 * LANES), bf16),
            vmem((RING, ROWS, 2 * LANES), bf16),
            vmem((RING, ROWS, 2 * LANES), bf16),
            vmem((RING, ROWS, 2 * LANES), bf16),
            vmem((GROUPS, 4, ROWS, 2 * LANES), bf16),
            vmem((GROUPS, 4, ROWS, 2 * LANES), bf16),
            vmem((2, 4, ROWS, 2 * LANES), bf16),
            vmem((GROUPS, 4, ROWS, 2 * LANES), bf16),
            vmem((LANES, 1280), f32),
            vmem((LANES, 768), f32),
            vmem((COARSE_C, LANES), f32),
            vmem((COARSE_C, LANES), f32),
            vmem((2, 4, ROWS, LANES), bf16),
            vmem((GROUPS, 4, ROWS, LANES), bf16),
            vmem((LANES, 2 * L1), f32),
            vmem((FINE_C, LANES), f32),
            vmem((FINE_C, LANES), f32),
            dma((2, 2)),
            dma((2, 2)),
            dma((2, 2, 5)),
            dma((2, 2, 5)),
            dma((2, 2, 5, 2)),
            dma((2, 2, 5, 2)),
            dma((1,)),
            dma((1,)),
            dma((2, RING)),
            dma((2, RING)),
            dma((4,)),
            dma((4,)),
            dma((4, GROUPS)),
            dma((4, GROUPS)),
        ],
        compiler_params=pltpu.CompilerParams(
            collective_id=0, has_side_effects=True, vmem_limit_bytes=56 * 1024 * 1024
        ),
    )(enc[0], cot[0], w1, w2)
    return merged[None], grad_enc[None]


def solution(mesh):
    placed = P(None, "tp", "ctx")
    return jax.shard_map(
        shards,
        mesh=mesh,
        in_specs=(placed,) * 4,
        out_specs=(placed, placed),
        check_vma=False,
    )
```

time: 381 us -> 126 us (0.33); the launches traced: 375 us -> 125 us
  waiting for transfers between devices: 248 us -> 0 us
  Pallas kernels: 0 us -> 119 us
  local copies, waits for them, and re-layouts: 59.1 us -> 4.91 us
  starting transfers between devices: 20.5 us -> 0 us
  blocking collectives: 16 us -> 0 us
  matrix products: 15.4 us -> 0 us
  between operations: 14.4 us -> 0.71 us
    all_gather x3 -> x0, waiting for transfers between devices: 197 us -> none  [the longest x1 84.4 us: shards(): lax.all_gather(w_up, 'ctx', axis=2, tiled=True)]
    pallas_call x0 -> x1, Pallas kernels: none -> 119 us  [shards(): pl.pallas_call(kernel, out_shape=[jax.ShapeDtypeStruct((FINE_C, FINE), bf...]
    unnamed x7 -> x0, waiting for transfers between devices: 41.4 us -> none
    unnamed x50 -> x8, local copies, waits for them, and re-layouts: 36.1 us -> 2.47 us
    ppermute x8 -> x0, starting transfers between devices: 20.3 us -> none  [the longest x4 14.9 us: with_halo(): lax.ppermute(tail, axis, [(i, (i + 1) % count) for i in range(ends)])]
    slice x5 -> x4, local copies, waits for them, and re-layouts: 19.4 us -> 0.85 us  [the longest x2 0.82 us: shards(): odd = up[:, 1::2].reshape(OUT2, 2 * COARSE_C)]
    all_gather x1 -> x0, blocking collectives: 16 us -> none  [shards(): coarse_all = lax.all_gather(grad_coarse, 'tp', axis=1, tiled=True)]
    dot_general x20 -> x0, matrix products: 15.4 us -> none  [the longest x10 7.53 us: back_terms(): jnp.einsum('bol,co->bcl', window, taps[offset], preferred_element_type=jn...]
  transfers between devices with their start and end apart: 13 -> 0, of which waited for: 7 -> 0; matrix products, arithmetic and copies ran while one was open for 14% -> 0% of each run, Pallas kernels for 0% -> 0%
where the time goes in v1:
time: 126 us; the launch traced here: 125 us
  Pallas kernels  119 us (94%)
  local copies, waits for them, and re-layouts  4.91 us (4%)
    pallas_call x1, Pallas kernels, shards(): pl.pallas_call(kernel, out_shape=[jax.ShapeDtypeStruct((FINE_C, FINE), bf...  119 us

profile of v1, /device:TPU:1, one launch (start us, length us, event | category | flops | bytes accessed | tf_op | source)
XLA Modules:
  0.0 124.6 jit_solution(10581670687732028535)
XLA Ops:
  0.6 0.0 copy-start.1
  0.6 0.8 slice.7
  1.5 0.1 reshape.15
  1.6 0.0 copy-done.1
  1.6 0.1 reshape.14
  1.7 0.0 copy-start.2
  1.7 0.6 pad.14.w2_ref
  2.4 0.2 copy-done.2
  2.6 0.1 reshape.13
  2.7 0.6 pad.12.w1_ref
  3.3 119.0 %shard_map.59 = (bf16[176,384]{1,0:T(8,128)(2,1)}, bf16[176,384]{1,0:T(8,128)(2,1)}) custom-call(bf16[176,384]{1,0:T(8,128)(2,1)} %bitcast.8, bf16[176,384]{1,0:T(8,128)(2,1)} %bitcast.9, bf16[24,896]{1,0:T(8,128)(2,1)} %pad.12.w1_ref, bf16[24,1024]{1,0:T(8,128)(2,1)} %pad.14.w2_ref), custom_call_target="tpu_custom_call" | custom-call | tf_op jit(solution)/shard_map/pallas_call | solution.py:457
  122.3 0.0 copy-start
  122.3 1.6 %copy.14 = bf16[1,176,384]{2,1,0:T(8,128)(2,1)} copy(bf16[1,176,384]{2,1,0:T(8,128)(2,1)} %bitcast.7) | data formatting | bytes 270336
  123.9 0.0 copy-done
  123.9 0.7 copy.15
  (5 shorter events, 0.1 us)
Async XLA Ops:
  0.6 0.9 copy-start.1
  1.7 0.8 copy-start.2
  122.3 1.6 %copy-start = (bf16[176,384]{1,0:T(8,128)(2,1)S(1)}, bf16[176,384]{1,0:T(8,128)(2,1)}, u32[]{:S(2)}) copy-start(bf16[176,384]{1,0:T(8,128)(2,1)} %get-tuple-element.5) | copy-start | bytes 405508

commit v2 on v1

v2 whole, which is shorter than its diff:
```python
import functools

import jax
import jax.numpy as jnp
from jax import lax
from jax.experimental import pallas as pl
from jax.experimental.pallas import tpu as pltpu
from jax.sharding import PartitionSpec as P

MESH = pl.DeviceIdType.MESH
bf16 = jnp.bfloat16
f32 = jnp.float32
root_half = 0.7071067811865476
norm_scale = 0.3989422804014327

RING = 8
GROUPS = 8
FINE_C, COARSE_C = 176, 192
OUT1, OUT2 = 24, 22
ROWS = 24
L1, L2 = 896, 1024
POS, LANES, EDGE = 192, 256, 32
FINE = 384
WIDE = 128 + FINE + 128


def erf(value):
    return lax.erf(value)


def gelu_value(value):
    return 0.5 * value * (1.0 + erf(value * root_half))


def gelu_both(value):
    cumulative = 0.5 * (1.0 + erf(value * root_half))
    return value * cumulative, cumulative + value * jnp.exp(-0.5 * value * value) * norm_scale


def gelu_slope(value):
    return gelu_both(value)[1]


def dot(a, b):
    return jnp.dot(a, b, preferred_element_type=f32)


def dot_first(a, b):
    return lax.dot_general(a, b, (((0,), (0,)), ((), ())), preferred_element_type=f32)


def iota(shape, dim):
    return lax.broadcasted_iota(jnp.int32, shape, dim)


def flat(block):
    lanes = block.shape[-1]
    return block.reshape(RING * ROWS, lanes)


def transposed(value, width):
    if width < LANES:
        value = jnp.concatenate([value, jnp.zeros((LANES, LANES - width), f32)], axis=1)
    return jnp.transpose(value)[:width]


def shift(value, amount, axis):
    size = value.shape[axis]
    return value if amount % size == 0 else pltpu.roll(value, amount % size, axis=axis)


def kernel(
    enc_ref, cot_ref, w1_ref, w2_ref, merged_ref, genc_ref,
    enc_wide, cot_wide, w1_all, w1_swap, w2_all, w2_swap,
    pooled_own, pooled_other, x1, p1_send, p1_recv, pre_c, slope_c, c_own, c_other, x2,
    enc_rows, cot_rows, merged_rows, p2_send, p2_recv, g_send, g_recv, y1, y2, gc_out, gc_in,
    gc_send, gc_recv, y4, gp_out, gp_in,
    halo_s, halo_r, near_s, near_r, first_s, first_r, second_s, second_r, swap_s, swap_r,
    pair_s, pair_r, tp_s, tp_r,
):
    ctx, t = lax.axis_index("ctx"), lax.axis_index("tp")
    core = lax.rem(t, 2)
    mate = t + 1 - 2 * core
    z, y = lax.div(ctx, RING), lax.rem(ctx, RING)
    one = z + (y - z) * core
    two = y + (z - y) * core

    def ring(index, step):
        return lax.rem(index + RING + step, RING)

    def place(i, j):
        straight, crossed = i * RING + j, j * RING + i
        return straight + (crossed - straight) * core

    def remote(src, dst, send, recv, device):
        return pltpu.make_async_remote_copy(
            src_ref=src, dst_ref=dst, send_sem=send, recv_sem=recv, device_id=device, device_id_type=MESH
        )

    first_to = ((place(ring(one, 1), two), t), (place(ring(one, -1), two), t))
    second_to = ((place(one, ring(two, 1)), t), (place(one, ring(two, -1)), t))
    count = RING * RING
    ctx_next, ctx_prev = lax.rem(ctx + 1, count), lax.rem(ctx + count - 1, count)

    barrier = pltpu.get_barrier_semaphore()
    partners = [(place(ring(one, d), two), t) for d in range(1, RING)]
    partners += [*second_to, (ctx_next, t), (ctx_prev, t)]
    partners += [(ctx, lax.rem(t + d, GROUPS)) for d in range(1, GROUPS)]
    for device in partners:
        pl.semaphore_signal(barrier, inc=1, device_id=device, device_id_type=MESH)

    taps = ((w1_all, w1_swap), (w2_all, w2_swap))
    down = jnp.concatenate([w1_ref[k] for k in range(5)] + [jnp.zeros((16, OUT1), bf16)], axis=0).astype(f32)
    up = jnp.concatenate(
        [w2_ref[0], w2_ref[2], w2_ref[4], jnp.zeros((64, OUT2), bf16), w2_ref[1], w2_ref[3]], axis=0
    ).astype(f32)
    for w_all, tall in ((w1_all, down), (w2_all, up)):
        tall = jnp.concatenate([tall, jnp.zeros((tall.shape[0], 128 - tall.shape[1]), f32)], axis=1)
        w_all[two, lax.div(one, 2), lax.rem(one, 2)] = jnp.transpose(tall)[0:ROWS].astype(bf16)
    enc_wide[:, 128 : 128 + FINE] = enc_ref[...]
    cot_wide[:, 128 : 128 + FINE] = cot_ref[...]
    pl.semaphore_wait(barrier, len(partners))

    def halo(n, side):
        source, wide = ((enc_ref, enc_wide), (cot_ref, cot_wide))[n]
        if side == 0:
            src, dst, to = source.at[:, FINE - 128 : FINE], wide.at[:, 0:128], ctx_next
        else:
            src, dst, to = source.at[:, 0:128], wide.at[:, 128 + FINE : WIDE], ctx_prev
        return remote(src, dst, halo_s.at[n, side], halo_r.at[n, side], (to, t))

    def near(d):
        block = w1_all.at[two, lax.div(one, 2), lax.rem(one, 2)]
        return remote(block, block, near_s.at[d], near_r.at[d], (place(ring(one, d), two), t))

    def near_arrives(j):
        d = ring(one, -j)
        block = w1_all.at[two, lax.div(j, 2), lax.rem(j, 2)]
        remote(block, block, near_s.at[d], near_r.at[d], (place(ring(one, d), two), t)).wait_recv()

    def first(side, hop, arriving=False):
        step = hop if arriving else hop - 1
        index = ring(one, -step if side == 0 else step)
        block = w2_all.at[two, lax.div(index, 2), lax.rem(index, 2)]
        return remote(block, block, first_s.at[side, hop], first_r.at[side, hop], first_to[side])

    def piece(n):
        return lax.rem(lax.div(one, 2) + (0, 1, 3, 2)[n], 4)

    def second(w, side, hop, n, arriving=False):
        step = hop if arriving else hop - 1
        index = ring(two, -step if side == 0 else step)
        block = taps[w][0].at[index, piece(n)]
        return remote(block, block, second_s.at[w, side, hop, n], second_r.at[w, side, hop, n], second_to[side])

    def swap_zero(w, index):
        return remote(
            taps[w][0].at[index], taps[w][1].at[lax.div(index, 2)],
            swap_s.at[w, lax.div(index, 2)], swap_r.at[w, lax.div(index, 2)], (ctx, mate),
        )

    def swap_one(w, index):
        return remote(
            taps[w][0].at[index, :, 0], taps[w][1].at[:, lax.div(index, 2), lax.rem(index, 2)],
            swap_s.at[w, index], swap_r.at[w, index], (ctx, mate),
        )

    def swap(w, index):
        @pl.when(jnp.logical_and(core == 0, lax.rem(index, 2) == 1))
        def _():
            swap_zero(w, index).start()

        @pl.when(core == 1)
        def _():
            swap_one(w, index).start()

    def swap_done(w):
        @pl.when(core == 0)
        def _():
            for index in range(RING):
                swap_one(w, index).wait_recv()

        @pl.when(core == 1)
        def _():
            for index in range(1, RING, 2):
                swap_zero(w, index).wait_recv()

    def swap_sent(w):
        @pl.when(core == 0)
        def _():
            for index in range(1, RING, 2):
                swap_zero(w, index).wait_send()

        @pl.when(core == 1)
        def _():
            for index in range(RING):
                swap_one(w, index).wait_send()

    hops_first = {0: 4, 1: 3}

    def first_step(hop):
        for side in (0, 1):
            if hop <= hops_first[side]:
                if hop > 0:
                    first(side, hop, True).wait_recv()
                if hop < hops_first[side]:
                    first(side, hop + 1).start()

    def last_side(n):
        return 0 if n < 2 else 1

    def second_start(w, n):
        for side in (0, 1):
            second(w, side, 1, n).start()

    def second_step(w, hop):
        if hop < 4:
            for n in range(4):
                for side in (0, 1):
                    second(w, side, hop, n, True).wait_recv()
                    if hop < 3 or side == last_side(n):
                        second(w, side, hop + 1, n).start()
            swap(w, ring(two, hop))
            swap(w, ring(two, -hop))
        else:
            for n in range(4):
                second(w, last_side(n), 4, n, True).wait_recv()
            swap(w, ring(two, 4))

    def pair(n, src, dst):
        return remote(src, dst, pair_s.at[n], pair_r.at[n], (ctx, mate))

    def to_group(n, d, src, dst):
        return remote(src, dst, tp_s.at[n, d], tp_r.at[n, d], (ctx, lax.rem(t + d, GROUPS)))

    def scatter(n, c, send, recv, d):
        part = pl.ds(2 * c, 2)
        return to_group(n + c, d, send.at[lax.rem(t + d, GROUPS), part], recv.at[t, part])

    def gather(n, c, send, recv, d):
        part = pl.ds(2 * c, 2)
        return to_group(n + c, d, send.at[lax.rem(lax.rem(t + d, GROUPS), 2), part], recv.at[t, part])

    order = (4, 3, 5, 2, 6, 1, 7)

    def with_taps(w, q, use):
        w_all, w_swap = taps[w]

        @pl.when(core == 0)
        def _():
            use(flat(w_all[2 * q]), flat(w_swap[q]))

        @pl.when(core == 1)
        def _():
            use(flat(w_all[:, q, 1]), flat(w_swap[q]))

    for d in (1, 7, 2, 6, 3, 5, 4):
        near(d).start()
    near_arrives(one + 1 - 2 * lax.rem(one, 2))
    second_start(0, 0)
    for n in (1, 2, 3):
        near_arrives(2 * piece(n))
        near_arrives(2 * piece(n) + 1)
        second_start(0, n)
    swap(0, two)
    first_step(0)
    for n in (0, 1):
        for side in (0, 1):
            halo(n, side).start()

    lane = iota((WIDE, 2 * LANES), 1)
    row = iota((WIDE, 2 * LANES), 0)
    half_lane = lax.rem(lane, LANES)
    pick = jnp.where(row == 2 * half_lane + 64 + lax.div(lane, LANES), 1.0, 0.0).astype(bf16)
    where_to = iota((RING * ROWS, FINE_C), 1)
    spread = jnp.where(
        iota((RING * ROWS, FINE_C), 0) == lax.div(where_to, OUT2) * ROWS + lax.rem(where_to, OUT2), 1.0, 0.0
    ).astype(bf16)
    at = ctx * POS + iota((1, LANES), 1) - EDGE
    inside = jnp.logical_and(at >= 0, at < count * POS)
    second_step(0, 1)
    first_step(1)
    for n in (0, 1):
        for side in (0, 1):
            halo(n, side).wait_recv()
    enc_ed = dot(enc_wide[...], pick)
    pooled = jnp.where(inside, (enc_ed[:, 0:LANES] + enc_ed[:, LANES:]) * 0.5, 0.0)
    pooled_own[...] = pooled.astype(bf16)
    pair(0, pooled_own, pooled_other).start()
    second_step(0, 2)
    first_step(2)
    enc_rows[...] = dot(spread, enc_ed.astype(bf16)).reshape(RING, ROWS, 2 * LANES).astype(bf16)
    cot_ed = dot(cot_wide[...], pick).astype(bf16)
    cot_rows[...] = dot(spread, cot_ed).reshape(RING, ROWS, 2 * LANES).astype(bf16)
    pair(0, pooled_own, pooled_other).wait_recv()
    for other, ref in enumerate((pooled_own, pooled_other)):
        value = ref[...].astype(f32)
        for k in range(5):
            start = other * L1 + k * FINE_C
            x1[start : start + FINE_C] = shift(value, 2 - k, 1).astype(bf16)
        x1[other * L1 + 880 : (other + 1) * L1] = jnp.zeros((16, LANES), bf16)
    second_step(0, 3)
    first_step(3)
    first_step(4)
    for n in range(4):
        second_start(1, n)
    swap(1, two)
    second_step(0, 4)
    swap_done(0)

    for c in (0, 1):

        @pl.loop(2 * c, 2 * c + 2)
        def _(q):
            def use(mine, swapped):
                part = dot(mine, x1[0:L1]) + dot(swapped, x1[L1 : 2 * L1])
                p1_send[:, q] = part.reshape(RING, ROWS, LANES).astype(bf16)

            with_taps(0, q, use)

        for d in order:
            scatter(0, c, p1_send, p1_recv, d).start()

    p1_recv[t] = p1_send[t]
    second_step(1, 1)
    second_step(1, 2)
    for c in (0, 1):
        for d in order:
            scatter(0, c, p1_send, p1_recv, d).wait_recv()
    sides = [sum(p1_recv[2 * x + p].astype(f32) for x in range(4)) for p in (0, 1)]
    pre_c[...] = jnp.stack(sides, axis=1).reshape(COARSE_C, LANES)
    c_own[...] = jnp.where(inside, gelu_value(pre_c[...]), 0.0).astype(bf16)
    pair(1, c_own, c_other).start()
    slope_c[...] = gelu_slope(pre_c[...])
    pair(1, c_own, c_other).wait_recv()
    for other, ref in enumerate((c_own, c_other)):
        value = ref[...]
        wide = value.astype(f32)
        before, after = shift(wide, 1, 1).astype(bf16), shift(wide, -1, 1).astype(bf16)
        for start, even, odd in (
            (0, before, before),
            (192, value, value),
            (384, after, after),
            (640, before, value),
            (832, value, after),
        ):
            start += other * L2
            x2[start : start + COARSE_C, 0:LANES] = even
            x2[start : start + COARSE_C, LANES : 2 * LANES] = odd
        x2[other * L2 + 576 : other * L2 + 640] = jnp.zeros((64, 2 * LANES), bf16)
    second_step(1, 3)
    second_step(1, 4)
    swap_done(1)

    for c in (0, 1):

        @pl.loop(2 * c, 2 * c + 2)
        def _(q):
            def use(mine, swapped):
                part = dot(mine, x2[0:L2]) + dot(swapped, x2[L2 : 2 * L2])
                p2_send[:, q] = part.reshape(RING, ROWS, 2 * LANES).astype(bf16)

            with_taps(1, q, use)

        for d in order:
            scatter(2, c, p2_send, p2_recv, d).start()

    p2_recv[t] = p2_send[t]
    for c in (0, 1):
        for d in order:
            scatter(2, c, p2_send, p2_recv, d).wait_recv()

        @pl.loop(2 * c, 2 * c + 2)
        def _(q):
            for p in (0, 1):
                pre = sum(p2_recv[2 * x + p, q].astype(f32) for x in range(4))
                value, slope = gelu_both(pre)
                merged_rows[2 * q + p] = (enc_rows[2 * q + p].astype(f32) + value).astype(bf16)
                grad = (cot_rows[2 * q + p].astype(f32) * slope).astype(bf16).astype(f32)
                even = jnp.where(inside, grad[:, 0:LANES], 0.0)
                odd = jnp.where(inside, grad[:, LANES:], 0.0)
                g_send[p, q, :, 0:LANES] = (even + odd).astype(bf16)
                g_send[p, q, :, LANES : 2 * LANES] = (even + shift(odd, 1, 1)).astype(bf16)

        for d in order:
            gather(4, c, g_send, g_recv, d).start()
    g_recv[t] = g_send[core]

    back = iota((2 * LANES, FINE), 1)
    unpick = jnp.where(
        iota((2 * LANES, FINE), 0) == lax.rem(back, 2) * LANES + lax.div(back, 2) + EDGE, 1.0, 0.0
    ).astype(bf16)
    kept = dot_first(spread, flat(merged_rows[...])).astype(bf16)
    merged_ref[...] = dot(kept, unpick).astype(bf16)

    for c in (0, 1):
        for d in order:
            gather(4, c, g_send, g_recv, d).wait_recv()

        def add(mine, swapped, q):
            block = flat(g_recv[:, q])
            for other, use in enumerate((mine, swapped)):
                sums = dot_first(block[:, 0:LANES], use[:, 0:640])
                pairs = dot_first(block[:, LANES:], use[:, 640:1024])
                if q == 0:
                    y1[other], y2[other] = sums, pairs
                else:
                    y1[other] += sums
                    y2[other] += pairs

        for q in (2 * c, 2 * c + 1):
            with_taps(1, q, functools.partial(add, q=q))

    def coarse_part(other):
        total = shift(y1[other, :, 0:192] + y2[other, :, 0:192], -1, 0)
        total = total + y1[other, :, 192:384] + y2[other, :, 192:384]
        total = total + shift(y1[other, :, 384:576], 1, 0)
        return transposed(total, COARSE_C)

    gc_out[...] = coarse_part(1)
    pair(2, gc_out, gc_in).start()
    own = coarse_part(0)
    pair(2, gc_out, gc_in).wait_recv()
    grad_c = jnp.where(inside, (own + gc_in[...]) * slope_c[...], 0.0).reshape(4, 2, ROWS, LANES).astype(bf16)
    gc_send[0] = grad_c[:, 0]
    gc_send[1] = grad_c[:, 1]
    for c in (0, 1):
        for d in order:
            gather(6, c, gc_send, gc_recv, d).start()
    gc_recv[t] = gc_send[core]
    coarse_row = iota((LANES, FINE), 0)
    widen = jnp.where(coarse_row == lax.div(iota((LANES, FINE), 1), 2) + EDGE, 1.0, 0.0).astype(bf16)
    for c in (0, 1):
        for d in order:
            gather(6, c, gc_send, gc_recv, d).wait_recv()

        def add(mine, swapped, q):
            block = flat(gc_recv[:, q])
            for other, use in enumerate((mine, swapped)):
                if q == 0:
                    y4[other] = dot_first(block, use)
                else:
                    y4[other] += dot_first(block, use)

        for q in (2 * c, 2 * c + 1):
            with_taps(0, q, functools.partial(add, q=q))

    def fine_part(other):
        total = None
        for k in range(5):
            term = shift(y4[other, :, k * FINE_C : (k + 1) * FINE_C], k - 2, 0)
            total = term if total is None else total + term
        return transposed(total, FINE_C)

    gp_out[...] = fine_part(1)
    pair(3, gp_out, gp_in).start()
    own = fine_part(0)
    pair(3, gp_out, gp_in).wait_recv()
    total = (own + gp_in[...]) * 0.5
    high = total.astype(bf16)
    low = (total - high.astype(f32)).astype(bf16)
    genc_ref[...] = (cot_ref[...].astype(f32) + dot(high, widen) + dot(low, widen)).astype(bf16)

    for n in (0, 1):
        for side in (0, 1):
            halo(n, side).wait_send()
    for d in range(1, RING):
        near(d).wait_send()
    for side in (0, 1):
        for hop in range(1, hops_first[side] + 1):
            first(side, hop).wait_send()
    for w in (0, 1):
        for side in (0, 1):
            for n in range(4):
                for hop in (1, 2, 3, 4):
                    if hop < 4 or side == last_side(n):
                        second(w, side, hop, n).wait_send()
        swap_sent(w)
    pair(0, pooled_own, pooled_other).wait_send()
    pair(1, c_own, c_other).wait_send()
    pair(2, gc_out, gc_in).wait_send()
    pair(3, gp_out, gp_in).wait_send()
    for c in (0, 1):
        for d in order:
            scatter(0, c, p1_send, p1_recv, d).wait_send()
            scatter(2, c, p2_send, p2_recv, d).wait_send()
            gather(4, c, g_send, g_recv, d).wait_send()
            gather(6, c, gc_send, gc_recv, d).wait_send()


def shards(enc, w_down, w_up, cot):
    dma = pltpu.SemaphoreType.DMA
    vmem = pltpu.VMEM
    merged, grad_enc = pl.pallas_call(
        kernel,
        out_shape=[jax.ShapeDtypeStruct((FINE_C, FINE), bf16)] * 2,
        in_specs=[pl.BlockSpec(memory_space=vmem)] * 4,
        out_specs=[pl.BlockSpec(memory_space=vmem)] * 2,
        scratch_shapes=[
            vmem((FINE_C, WIDE), bf16),
            vmem((FINE_C, WIDE), bf16),
            vmem((RING, 4, 2, ROWS, L1), bf16),
            vmem((4, 4, 2, ROWS, L1), bf16),
            vmem((RING, 4, 2, ROWS, L2), bf16),
            vmem((4, 4, 2, ROWS, L2), bf16),
            vmem((FINE_C, LANES), bf16),
            vmem((FINE_C, LANES), bf16),
            vmem((2 * L1, LANES), bf16),
            vmem((GROUPS, 4, ROWS, LANES), bf16),
            vmem((GROUPS, 4, ROWS, LANES), bf16),
            vmem((COARSE_C, LANES), f32),
            vmem((COARSE_C, LANES), f32),
            vmem((COARSE_C, LANES), bf16),
            vmem((COARSE_C, LANES), bf16),
            vmem((2 * L2, 2 * LANES), bf16),
            vmem((RING, ROWS, 2 * LANES), bf16),
            vmem((RING, ROWS, 2 * LANES), bf16),
            vmem((RING, ROWS, 2 * LANES), bf16),
            vmem((GROUPS, 4, ROWS, 2 * LANES), bf16),
            vmem((GROUPS, 4, ROWS, 2 * LANES), bf16),
            vmem((2, 4, ROWS, 2 * LANES), bf16),
            vmem((GROUPS, 4, ROWS, 2 * LANES), bf16),
            vmem((2, LANES, 640), f32),
            vmem((2, LANES, 384), f32),
            vmem((COARSE_C, LANES), f32),
            vmem((COARSE_C, LANES), f32),
            vmem((2, 4, ROWS, LANES), bf16),
            vmem((GROUPS, 4, ROWS, LANES), bf16),
            vmem((2, LANES, L1), f32),
            vmem((FINE_C, LANES), f32),
            vmem((FINE_C, LANES), f32),
            dma((2, 2)),
            dma((2, 2)),
            dma((RING,)),
            dma((RING,)),
            dma((2, 5)),
            dma((2, 5)),
            dma((2, 2, 5, 4)),
            dma((2, 2, 5, 4)),
            dma((2, RING)),
            dma((2, RING)),
            dma((4,)),
            dma((4,)),
            dma((8, GROUPS)),
            dma((8, GROUPS)),
        ],
        compiler_params=pltpu.CompilerParams(
            collective_id=0, has_side_effects=True, vmem_limit_bytes=56 * 1024 * 1024
        ),
    )(enc[0], cot[0], w_down, w_up)
    return merged[None], grad_enc[None]


def solution(mesh):
    placed = P(None, "tp", "ctx")
    return jax.shard_map(
        shards,
        mesh=mesh,
        in_specs=(placed,) * 4,
        out_specs=(placed, placed),
        check_vma=False,
    )
```

time: 126 us -> 105 us (0.83)
  Pallas kernels: 119 us -> 98.9 us
    pallas_call x1, Pallas kernels: 119 us -> 98.9 us  [shards(): pl.pallas_call(kernel, out_shape=[jax.ShapeDtypeStruct((FINE_C, FINE), bf...]
    unnamed x8, local copies, waits for them, and re-layouts: 2.47 us -> 4.83 us
where the time goes in v2:
time: 105 us; the launch traced here: 104 us
  Pallas kernels  98.9 us (94%)
  local copies, waits for them, and re-layouts  4.83 us (5%)
    pallas_call x1, Pallas kernels, shards(): pl.pallas_call(kernel, out_shape=[jax.ShapeDtypeStruct((FINE_C, FINE), bf...  98.9 us
    unnamed x8, local copies, waits for them, and re-layouts  4.83 us

profile of v2, /device:TPU:1, one launch (start us, length us, event | category | flops | bytes accessed | tf_op | source)
XLA Modules:
  0.0 104.4 jit_solution(909970656938923766)
XLA Ops:
  0.6 0.0 copy-start.1
  0.6 1.7 %copy.6.w1_ref = bf16[5,176,24]{2,1,0:T(8,128)(2,1)} copy(bf16[5,176,24]{1,2,0:T(8,128)(2,1)} %param.5) | data formatting | bytes 84480 | tf_op args[1]
  2.3 0.0 copy-done.1
  2.3 0.9 copy.7.w2_ref
  3.2 98.9 %shard_map.59 = (bf16[176,384]{1,0:T(8,128)(2,1)}, bf16[176,384]{1,0:T(8,128)(2,1)}) custom-call(bf16[176,384]{1,0:T(8,128)(2,1)} %bitcast.6, bf16[176,384]{1,0:T(8,128)(2,1)} %bitcast.7, bf16[5,176,24]{2,1,0:T(8,128)(2,1)} %copy.6.w1_ref, bf16[5,192,22]{2,1,0:T(8,128)(2,1)} %copy.7.w2_ref), custom_call_target="tpu_custom_call" | custom-call | tf_op jit(solution)/shard_map/pallas_call | solution.py:494
  102.1 0.0 copy-start
  102.1 1.6 %copy.10 = bf16[1,176,384]{2,1,0:T(8,128)(2,1)} copy(bf16[1,176,384]{2,1,0:T(8,128)(2,1)} %bitcast.5) | data formatting | bytes 270336
  103.7 0.0 copy-done
  103.7 0.7 copy.11
Async XLA Ops:
  0.6 1.7 %copy-start.1 = (bf16[5,192,22]{1,2,0:T(8,128)(2,1)S(1)}, bf16[5,192,22]{1,2,0:T(8,128)(2,1)}, u32[]{:S(2)}) copy-start(bf16[5,192,22]{1,2,0:T(8,128)(2,1)} %param.6) | copy-start | bytes 126724
  102.1 1.6 %copy-start = (bf16[176,384]{1,0:T(8,128)(2,1)S(1)}, bf16[176,384]{1,0:T(8,128)(2,1)}, u32[]{:S(2)}) copy-start(bf16[176,384]{1,0:T(8,128)(2,1)} %get-tuple-element.5) | copy-start | bytes 405508

commit v3 on v2

v3 whole, which is shorter than its diff:
```python
import jax
import jax.numpy as jnp
from jax import lax
from jax.experimental import pallas as pl
from jax.experimental.pallas import tpu as pltpu
from jax.sharding import PartitionSpec as P

MESH = pl.DeviceIdType.MESH
bf16 = jnp.bfloat16
f32 = jnp.float32
root_half = 0.7071067811865476
norm_scale = 0.3989422804014327

RING = 8
GROUPS = 8
FINE_C, COARSE_C = 176, 192
OUT1, OUT2 = 24, 22
ROWS = 24
L1, L2 = 896, 1024
POS, LANES, EDGE = 192, 256, 32
FINE = 384
WIDE = 128 + FINE + 128
VMEM_LIMIT = 36 << 20


def erf(value):
    return lax.erf(value)


def gelu_value(value):
    return 0.5 * value * (1.0 + erf(value * root_half))


def gelu_both(value):
    cumulative = 0.5 * (1.0 + erf(value * root_half))
    return value * cumulative, cumulative + value * jnp.exp(-0.5 * value * value) * norm_scale


def gelu_slope(value):
    return gelu_both(value)[1]


def dot(a, b):
    return jnp.dot(a, b, preferred_element_type=f32)


def dot_first(a, b):
    return lax.dot_general(a, b, (((0,), (0,)), ((), ())), preferred_element_type=f32)


def iota(shape, dim):
    return lax.broadcasted_iota(jnp.int32, shape, dim)


def flat(block):
    lanes = block.shape[-1]
    return block.reshape(RING * ROWS, lanes)


def transposed(value, width):
    if width < LANES:
        value = jnp.concatenate([value, jnp.zeros((LANES, LANES - width), f32)], axis=1)
    return jnp.transpose(value)[:width]


def shift(value, amount, axis):
    size = value.shape[axis]
    return value if amount % size == 0 else pltpu.roll(value, amount % size, axis=axis)


def kernel(
    enc_ref, cot_ref, w1_ref, w2_ref, merged_ref, genc_ref,
    edge_out, edge_in, enc_wide, cot_wide, w1_all, w1_swap, w2_all, w2_swap,
    pooled_own, pooled_other, x1, p1_send, p1_recv, pre_c, slope_c, c_own, c_other, x2,
    enc_rows, cot_rows, merged_rows, p2_send, p2_recv, g_send, g_recv, y1, y2, gc_out, gc_in,
    gc_send, gc_recv, y4, gp_out, gp_in,
    halo_s, halo_r, near_s, near_r, first_s, first_r, second_s, second_r, swap_s, swap_r,
    pair_s, pair_r, tp_s, tp_r,
):
    ctx, t = lax.axis_index("ctx"), lax.axis_index("tp")
    core = lax.rem(t, 2)
    mate = t + 1 - 2 * core
    z, y = lax.div(ctx, RING), lax.rem(ctx, RING)
    one = z + (y - z) * core
    two = y + (z - y) * core

    def ring(index, step):
        return lax.rem(index + RING + step, RING)

    def place(i, j):
        straight, crossed = i * RING + j, j * RING + i
        return straight + (crossed - straight) * core

    def remote(src, dst, send, recv, device):
        return pltpu.make_async_remote_copy(
            src_ref=src, dst_ref=dst, send_sem=send, recv_sem=recv, device_id=device, device_id_type=MESH
        )

    second_to = ((place(one, ring(two, 1)), t), (place(one, ring(two, -1)), t))
    count = RING * RING
    ctx_next, ctx_prev = lax.rem(ctx + 1, count), lax.rem(ctx + count - 1, count)

    barrier = pltpu.get_barrier_semaphore()
    partners = [(place(ring(one, d), two), t) for d in range(1, RING)]
    partners += [*second_to, (ctx_next, t), (ctx_prev, t)]
    partners += [(ctx, lax.rem(t + d, GROUPS)) for d in range(1, GROUPS)]
    for device in partners:
        pl.semaphore_signal(barrier, inc=1, device_id=device, device_id_type=MESH)

    taps = ((w1_all, w1_swap), (w2_all, w2_swap))
    down = [w1_ref[k].astype(f32) for k in range(5)]
    up = [w2_ref[k].astype(f32) for k in range(5)]
    down = jnp.concatenate([*down, jnp.zeros((OUT1, 16), f32)], axis=1)
    up = jnp.concatenate([up[0], up[2], up[4], jnp.zeros((OUT2, 64), f32), up[1], up[3]], axis=1)
    up = jnp.concatenate([up, jnp.zeros((ROWS - OUT2, L2), f32)], axis=0)
    for w_all, block in ((w1_all, down), (w2_all, up)):
        w_all[two, lax.div(one, 2), lax.rem(one, 2)] = block.astype(bf16)
    enc_wide[:, 128 : 128 + FINE] = enc_ref[...]
    cot_wide[:, 128 : 128 + FINE] = cot_ref[...]
    low = iota((FINE_C, 128), 1) < 64
    last, first_tile = slice(FINE - 128, FINE), slice(0, 128)
    enc_last, cot_last = enc_ref[:, last].astype(f32), shift(cot_ref[:, last].astype(f32), 64, 1)
    enc_first, cot_first = enc_ref[:, first_tile].astype(f32), shift(cot_ref[:, first_tile].astype(f32), 64, 1)
    edge_out[0] = jnp.where(low, cot_last, enc_last).astype(bf16)
    edge_out[1] = jnp.where(low, enc_first, cot_first).astype(bf16)
    pl.semaphore_wait(barrier, len(partners))

    def halo(side):
        to = ctx_next if side == 0 else ctx_prev
        return remote(edge_out.at[side], edge_in.at[side], halo_s.at[side], halo_r.at[side], (to, t))

    def near(d):
        block = w1_all.at[two, lax.div(one, 2), lax.rem(one, 2)]
        return remote(block, block, near_s.at[d], near_r.at[d], (place(ring(one, d), two), t))

    def near_arrives(j):
        d = ring(one, -j)
        block = w1_all.at[two, lax.div(j, 2), lax.rem(j, 2)]
        remote(block, block, near_s.at[d], near_r.at[d], (place(ring(one, d), two), t)).wait_recv()

    routes = ((0, 1), (0, -1), (0, 2), (0, -2), (-2, 1), (-2, 2), (2, -1))

    def first(m, arriving=False):
        origin, step = routes[m]
        index = ring(one, origin - step if arriving else origin)
        block = w2_all.at[two, lax.div(index, 2), lax.rem(index, 2)]
        return remote(block, block, first_s.at[m], first_r.at[m], (place(ring(one, step), two), t))

    def piece(n):
        return lax.rem(lax.div(one, 2) + (0, 1, 3, 2)[n], 4)

    def second(w, side, hop, n, arriving=False):
        step = hop if arriving else hop - 1
        index = ring(two, -step if side == 0 else step)
        block = taps[w][0].at[index, piece(n)]
        return remote(block, block, second_s.at[w, side, hop, n], second_r.at[w, side, hop, n], second_to[side])

    def swap_zero(w, index):
        return remote(
            taps[w][0].at[index], taps[w][1].at[lax.div(index, 2)],
            swap_s.at[w, lax.div(index, 2)], swap_r.at[w, lax.div(index, 2)], (ctx, mate),
        )

    def swap_one(w, index):
        return remote(
            taps[w][0].at[index, :, 0], taps[w][1].at[:, lax.div(index, 2), lax.rem(index, 2)],
            swap_s.at[w, index], swap_r.at[w, index], (ctx, mate),
        )

    def swap(w, index):
        @pl.when(jnp.logical_and(core == 0, lax.rem(index, 2) == 1))
        def _():
            swap_zero(w, index).start()

        @pl.when(core == 1)
        def _():
            swap_one(w, index).start()

    def swap_done(w):
        @pl.when(core == 0)
        def _():
            for index in range(RING):
                swap_one(w, index).wait_recv()

        @pl.when(core == 1)
        def _():
            for index in range(1, RING, 2):
                swap_zero(w, index).wait_recv()

    def swap_sent(w):
        @pl.when(core == 0)
        def _():
            for index in range(1, RING, 2):
                swap_zero(w, index).wait_send()

        @pl.when(core == 1)
        def _():
            for index in range(RING):
                swap_one(w, index).wait_send()

    def last_side(n):
        return 0 if n < 2 else 1

    def second_start(w, n):
        for side in (0, 1):
            second(w, side, 1, n).start()

    def second_part(w, hop, n):
        for side in (0, 1):
            second(w, side, hop, n, True).wait_recv()
            if hop < 3 or side == last_side(n):
                second(w, side, hop + 1, n).start()

    def second_swap(w, hop):
        swap(w, ring(two, hop))
        swap(w, ring(two, -hop))

    def second_step(w, hop):
        if hop < 4:
            for n in range(4):
                second_part(w, hop, n)
            second_swap(w, hop)
        else:
            for n in range(4):
                second(w, last_side(n), 4, n, True).wait_recv()
            swap(w, ring(two, 4))

    def pair(n, src, dst):
        return remote(src, dst, pair_s.at[n], pair_r.at[n], (ctx, mate))

    def to_group(n, d, src, dst):
        return remote(src, dst, tp_s.at[n, d], tp_r.at[n, d], (ctx, lax.rem(t + d, GROUPS)))

    def scatter(n, c, send, recv, d):
        part = pl.ds(2 * c, 2)
        return to_group(n + c, d, send.at[lax.rem(t + d, GROUPS), part], recv.at[t, part])

    def gather(n, c, send, recv, d):
        part = pl.ds(2 * c, 2)
        return to_group(n + c, d, send.at[lax.rem(lax.rem(t + d, GROUPS), 2), part], recv.at[t, part])

    order = (4, 3, 5, 2, 6, 1, 7)

    far = ring(z, 4)
    rows_near = [ring(z, k) for k in range(-3, 4)]

    def column(parity, slot):
        return lax.rem(y + RING - 2 - lax.rem(y + parity, 2) + 2 * slot, RING)

    def conv_fine(blocks):
        mine, swapped = [], []
        for slot, i in blocks:
            q, upper, lower = lax.div(column(core, slot), 2), lax.div(i, 2), lax.rem(i, 2)
            at = (2 * q + (i - 2 * q) * core, upper + (q - upper) * core, lower + (1 - lower) * core)
            mine.append(w2_all[at].astype(f32))
            swapped.append(w2_swap[q, upper, lower].astype(f32))
        mine, swapped = (jnp.concatenate(part, axis=0).astype(bf16) for part in (mine, swapped))
        sums = dot(mine, x2[0:L2]) + dot(swapped, x2[L2 : 2 * L2])
        for n, (slot, i) in enumerate(blocks):
            p2_send[i, slot] = sums[n * ROWS : (n + 1) * ROWS].astype(bf16)

    def fine_swap_done(last):
        @pl.when(core == 0)
        def _():
            for i in (far,) if last else rows_near:
                swap_one(1, i).wait_recv()

        @pl.when(core == 1)
        def _():
            for slot in (3,) if last else (0, 1, 2):
                swap_zero(1, column(1, slot)).wait_recv()

    def fine_copy(n, d, send, recv, index, slots):
        return to_group(n, d, send.at[index, slots], recv.at[t, slots])

    early, late, whole = pl.ds(0, 3), pl.ds(3, 1), pl.ds(0, 4)

    def fine_sums(last, act):
        for d in order:
            target = lax.rem(t + d, GROUPS)

            @pl.when(target != far)
            def _():
                act(fine_copy(2 + last, d, p2_send, p2_recv, target, late if last else early))

            if last:

                @pl.when(target == far)
                def _():
                    act(fine_copy(3, d, p2_send, p2_recv, target, whole))

    def fine_grads(last, act, source):
        for d in order:
            target = lax.rem(t + d, GROUPS)
            origin = ring(t, -d) if source else t

            @pl.when(origin != far)
            def _():
                act(fine_copy(4 + last, d, g_send, g_recv, lax.rem(target, 2), late if last else early))

            if last:

                @pl.when(origin == far)
                def _():
                    act(fine_copy(5, d, g_send, g_recv, lax.rem(target, 2), whole))

    def begun(copy):
        copy.start()

    def arrived(copy):
        copy.wait_recv()

    def left(copy):
        copy.wait_send()

    def with_taps(w, q, use):
        w_all, w_swap = taps[w]

        @pl.when(core == 0)
        def _():
            use([flat(w_all[2 * n]) for n in q], [flat(w_swap[n]) for n in q])

        @pl.when(core == 1)
        def _():
            use([flat(w_all[:, n, 1]) for n in q], [flat(w_swap[n]) for n in q])

    for d in (1, 7, 2, 6, 3, 5, 4):
        near(d).start()
    near_arrives(one + 1 - 2 * lax.rem(one, 2))
    second_start(0, 0)
    for n in (1, 2, 3):
        near_arrives(2 * piece(n))
        near_arrives(2 * piece(n) + 1)
        second_start(0, n)
    swap(0, two)
    for m in range(4):
        first(m).start()
    for side in (0, 1):
        halo(side).start()

    lane = iota((WIDE, 2 * LANES), 1)
    row = iota((WIDE, 2 * LANES), 0)
    half_lane = lax.rem(lane, LANES)
    pick = jnp.where(row == 2 * half_lane + 64 + lax.div(lane, LANES), 1.0, 0.0).astype(bf16)
    where_to = iota((RING * ROWS, FINE_C), 1)
    spread = jnp.where(
        iota((RING * ROWS, FINE_C), 0) == lax.div(where_to, OUT2) * ROWS + lax.rem(where_to, OUT2), 1.0, 0.0
    ).astype(bf16)
    at = ctx * POS + iota((1, LANES), 1) - EDGE
    inside = jnp.logical_and(at >= 0, at < count * POS)
    second_step(0, 1)
    for m in (2, 3):
        first(m, True).wait_recv()
    for m in (4, 5, 6):
        first(m).start()
    for side in (0, 1):
        halo(side).wait_recv()
        lanes = slice(0, 128) if side == 0 else slice(128 + FINE, WIDE)
        enc_wide[:, lanes] = edge_in[side]
        cot_wide[:, lanes] = shift(edge_in[side].astype(f32), 64, 1).astype(bf16)
    enc_ed = dot(enc_wide[...], pick)
    pooled = jnp.where(inside, (enc_ed[:, 0:LANES] + enc_ed[:, LANES:]) * 0.5, 0.0)
    pooled_own[...] = pooled.astype(bf16)
    pair(0, pooled_own, pooled_other).start()
    second_step(0, 2)
    enc_rows[...] = dot(spread, enc_ed.astype(bf16)).reshape(RING, ROWS, 2 * LANES).astype(bf16)
    cot_ed = dot(cot_wide[...], pick).astype(bf16)
    cot_rows[...] = dot(spread, cot_ed).reshape(RING, ROWS, 2 * LANES).astype(bf16)
    pair(0, pooled_own, pooled_other).wait_recv()
    for other, ref in enumerate((pooled_own, pooled_other)):
        value = ref[...].astype(f32)
        for k in range(5):
            start = other * L1 + k * FINE_C
            x1[start : start + FINE_C] = shift(value, 2 - k, 1).astype(bf16)
        x1[other * L1 + 880 : (other + 1) * L1] = jnp.zeros((16, LANES), bf16)
    for m in (0, 1, 4, 5, 6):
        first(m, True).wait_recv()
    second_step(0, 3)
    for n in range(4):
        second_start(1, n)
    swap(1, two)
    second_step(0, 4)

    for c in (0, 1):
        second_part(1, 1, 2 * c)
        second_part(1, 1, 2 * c + 1)
        if c == 0:
            swap_done(0)

        @pl.loop(2 * c, 2 * c + 2)
        def _(q):
            def use(mine, swapped):
                part = dot(mine[0], x1[0:L1]) + dot(swapped[0], x1[L1 : 2 * L1])
                p1_send[:, q] = part.reshape(RING, ROWS, LANES).astype(bf16)

            with_taps(0, [q], use)

        for d in order:
            scatter(0, c, p1_send, p1_recv, d).start()

    p1_recv[t] = p1_send[t]
    second_swap(1, 1)
    second_step(1, 2)
    for c in (0, 1):
        for d in order:
            scatter(0, c, p1_send, p1_recv, d).wait_recv()
    sides = [sum(p1_recv[2 * x + p].astype(f32) for x in range(4)) for p in (0, 1)]
    pre_c[...] = jnp.stack(sides, axis=1).reshape(COARSE_C, LANES)
    c_own[...] = jnp.where(inside, gelu_value(pre_c[...]), 0.0).astype(bf16)
    pair(1, c_own, c_other).start()
    slope_c[...] = gelu_slope(pre_c[...])
    pair(1, c_own, c_other).wait_recv()
    for other, ref in enumerate((c_own, c_other)):
        value = ref[...]
        wide = value.astype(f32)
        before, after = shift(wide, 1, 1).astype(bf16), shift(wide, -1, 1).astype(bf16)
        for start, even, odd in (
            (0, before, before),
            (192, value, value),
            (384, after, after),
            (640, before, value),
            (832, value, after),
        ):
            start += other * L2
            x2[start : start + COARSE_C, 0:LANES] = even
            x2[start : start + COARSE_C, LANES : 2 * LANES] = odd
        x2[other * L2 + 576 : other * L2 + 640] = jnp.zeros((64, 2 * LANES), bf16)
    second_step(1, 3)
    fine_swap_done(0)
    for slot in range(3):
        conv_fine([(slot, i) for i in rows_near])
    fine_sums(0, begun)
    second_step(1, 4)
    fine_swap_done(1)
    conv_fine([(slot, far) for slot in range(4)])
    conv_fine([(3, i) for i in rows_near])
    fine_sums(1, begun)
    p2_recv[t] = p2_send[t]

    def fine_slot(slot):
        for p in (0, 1):
            pre = sum(p2_recv[2 * x + p, slot].astype(f32) for x in range(4))
            value, slope = gelu_both(pre)
            at = column(p, slot)
            merged_rows[at] = (enc_rows[at].astype(f32) + value).astype(bf16)
            grad = (cot_rows[at].astype(f32) * slope).astype(bf16).astype(f32)
            even = jnp.where(inside, grad[:, 0:LANES], 0.0)
            odd = jnp.where(inside, grad[:, LANES:], 0.0)
            g_send[p, slot, :, 0:LANES] = (even + odd).astype(bf16)
            g_send[p, slot, :, LANES : 2 * LANES] = (even + shift(odd, 1, 1)).astype(bf16)

    @pl.when(t != far)
    def _():
        for d in order:
            fine_copy(2, d, p2_send, p2_recv, t, early).wait_recv()
        pl.loop(0, 3)(fine_slot)
        for d in order:
            fine_copy(4, d, g_send, g_recv, lax.rem(lax.rem(t + d, GROUPS), 2), early).start()
        for d in order:
            fine_copy(3, d, p2_send, p2_recv, t, late).wait_recv()

    @pl.when(t == far)
    def _():
        for d in order:
            fine_copy(3, d, p2_send, p2_recv, t, whole).wait_recv()
        pl.loop(0, 3)(fine_slot)

    fine_slot(3)
    fine_grads(1, begun, False)
    g_recv[t] = g_send[core]
    for side in (0, 1):
        halo(side).wait_send()
    for d in range(1, RING):
        near(d).wait_send()
    for m in range(7):
        first(m).wait_send()
    for w in (0, 1):
        for side in (0, 1):
            for n in range(4):
                for hop in (1, 2, 3, 4):
                    if hop < 4 or side == last_side(n):
                        second(w, side, hop, n).wait_send()
        swap_sent(w)
    pair(0, pooled_own, pooled_other).wait_send()
    pair(1, c_own, c_other).wait_send()
    for c in (0, 1):
        for d in order:
            scatter(0, c, p1_send, p1_recv, d).wait_send()
    back = iota((2 * LANES, FINE), 1)
    unpick = jnp.where(
        iota((2 * LANES, FINE), 0) == lax.rem(back, 2) * LANES + lax.div(back, 2) + EDGE, 1.0, 0.0
    ).astype(bf16)
    kept = dot_first(spread, flat(merged_rows[...])).astype(bf16)
    merged_ref[...] = dot(kept, unpick).astype(bf16)

    fine_grads(0, arrived, True)
    fine_grads(1, arrived, True)
    for c in (0, 1):
        columns = [lax.div(column(core, 2 * c + n), 2) for n in (0, 1)]
        block = jnp.concatenate([flat(g_recv[:, 2 * c + n]) for n in (0, 1)], axis=0)

        def add(mine, swapped):
            for other, use in enumerate((mine, swapped)):
                use = jnp.concatenate(use, axis=0)
                sums = dot_first(block[:, 0:LANES], use[:, 0:640])
                pairs = dot_first(block[:, LANES:], use[:, 640:1024])
                if c == 0:
                    y1[other], y2[other] = sums, pairs
                else:
                    y1[other] += sums
                    y2[other] += pairs

        with_taps(1, columns, add)

    def coarse_part(other):
        total = shift(y1[other, :, 0:192] + y2[other, :, 0:192], -1, 0)
        total = total + y1[other, :, 192:384] + y2[other, :, 192:384]
        total = total + shift(y1[other, :, 384:576], 1, 0)
        return transposed(total, COARSE_C)

    gc_out[...] = coarse_part(1)
    pair(2, gc_out, gc_in).start()
    own = coarse_part(0)
    pair(2, gc_out, gc_in).wait_recv()
    grad_c = jnp.where(inside, (own + gc_in[...]) * slope_c[...], 0.0).reshape(4, 2, ROWS, LANES).astype(bf16)
    gc_send[0] = grad_c[:, 0]
    gc_send[1] = grad_c[:, 1]
    for c in (0, 1):
        for d in order:
            gather(6, c, gc_send, gc_recv, d).start()
    gc_recv[t] = gc_send[core]
    pair(2, gc_out, gc_in).wait_send()
    for last in (0, 1):
        fine_sums(last, left)
        fine_grads(last, left, False)
    coarse_row = iota((LANES, FINE), 0)
    widen = jnp.where(coarse_row == lax.div(iota((LANES, FINE), 1), 2) + EDGE, 1.0, 0.0).astype(bf16)
    for c in (0, 1):
        for d in order:
            gather(6, c, gc_send, gc_recv, d).wait_recv()

        block = jnp.concatenate([flat(gc_recv[:, 2 * c + n]) for n in (0, 1)], axis=0)

        def add(mine, swapped):
            for other, use in enumerate((mine, swapped)):
                part = dot_first(block, jnp.concatenate(use, axis=0))
                if c == 0:
                    y4[other] = part
                else:
                    y4[other] += part

        with_taps(0, [2 * c, 2 * c + 1], add)

    def fine_part(other):
        total = None
        for k in range(5):
            term = shift(y4[other, :, k * FINE_C : (k + 1) * FINE_C], k - 2, 0)
            total = term if total is None else total + term
        return transposed(total, FINE_C)

    gp_out[...] = fine_part(1)
    pair(3, gp_out, gp_in).start()
    own = fine_part(0)
    for c in (0, 1):
        for d in order:
            gather(6, c, gc_send, gc_recv, d).wait_send()
    pair(3, gp_out, gp_in).wait_recv()
    total = (own + gp_in[...]) * 0.5
    high = total.astype(bf16)
    low = (total - high.astype(f32)).astype(bf16)
    genc_ref[...] = (cot_ref[...].astype(f32) + dot(high, widen) + dot(low, widen)).astype(bf16)

    pair(3, gp_out, gp_in).wait_send()


def shards(enc, w_down, w_up, cot):
    dma = pltpu.SemaphoreType.DMA
    vmem = pltpu.VMEM
    merged, grad_enc = pl.pallas_call(
        kernel,
        out_shape=[jax.ShapeDtypeStruct((FINE_C, FINE), bf16)] * 2,
        in_specs=[pl.BlockSpec(memory_space=vmem)] * 4,
        out_specs=[pl.BlockSpec(memory_space=vmem)] * 2,
        scratch_shapes=[
            vmem((2, FINE_C, 128), bf16),
            vmem((2, FINE_C, 128), bf16),
            vmem((FINE_C, WIDE), bf16),
            vmem((FINE_C, WIDE), bf16),
            vmem((RING, 4, 2, ROWS, L1), bf16),
            vmem((4, 4, 2, ROWS, L1), bf16),
            vmem((RING, 4, 2, ROWS, L2), bf16),
            vmem((4, 4, 2, ROWS, L2), bf16),
            vmem((FINE_C, LANES), bf16),
            vmem((FINE_C, LANES), bf16),
            vmem((2 * L1, LANES), bf16),
            vmem((GROUPS, 4, ROWS, LANES), bf16),
            vmem((GROUPS, 4, ROWS, LANES), bf16),
            vmem((COARSE_C, LANES), f32),
            vmem((COARSE_C, LANES), f32),
            vmem((COARSE_C, LANES), bf16),
            vmem((COARSE_C, LANES), bf16),
            vmem((2 * L2, 2 * LANES), bf16),
            vmem((RING, ROWS, 2 * LANES), bf16),
            vmem((RING, ROWS, 2 * LANES), bf16),
            vmem((RING, ROWS, 2 * LANES), bf16),
            vmem((GROUPS, 4, ROWS, 2 * LANES), bf16),
            vmem((GROUPS, 4, ROWS, 2 * LANES), bf16),
            vmem((2, 4, ROWS, 2 * LANES), bf16),
            vmem((GROUPS, 4, ROWS, 2 * LANES), bf16),
            vmem((2, LANES, 640), f32),
            vmem((2, LANES, 384), f32),
            vmem((COARSE_C, LANES), f32),
            vmem((COARSE_C, LANES), f32),
            vmem((2, 4, ROWS, LANES), bf16),
            vmem((GROUPS, 4, ROWS, LANES), bf16),
            vmem((2, LANES, L1), f32),
            vmem((FINE_C, LANES), f32),
            vmem((FINE_C, LANES), f32),
            dma((2,)),
            dma((2,)),
            dma((RING,)),
            dma((RING,)),
            dma((7,)),
            dma((7,)),
            dma((2, 2, 5, 4)),
            dma((2, 2, 5, 4)),
            dma((2, RING)),
            dma((2, RING)),
            dma((4,)),
            dma((4,)),
            dma((8, GROUPS)),
            dma((8, GROUPS)),
        ],
        compiler_params=pltpu.CompilerParams(
            collective_id=0, has_side_effects=True, vmem_limit_bytes=VMEM_LIMIT
        ),
    )(enc[0], cot[0], jnp.swapaxes(w_down, 1, 2), jnp.swapaxes(w_up, 1, 2))
    return merged[None], grad_enc[None]


def solution(mesh):
    placed = P(None, "tp", "ctx")
    return jax.shard_map(
        shards,
        mesh=mesh,
        in_specs=(placed,) * 4,
        out_specs=(placed, placed),
        check_vma=False,
    )
```

time: 105 us -> 98.4 us (0.937)
  Pallas kernels: 98.9 us -> 92.8 us
    pallas_call x1, Pallas kernels: 98.9 us -> 92.8 us  [shards(): pl.pallas_call(kernel, out_shape=[jax.ShapeDtypeStruct((FINE_C, FINE), bf...]
    unnamed x8 -> x10, local copies, waits for them, and re-layouts: 4.83 us -> 4.78 us
where the time goes in v3:
time: 98.4 us; the launch traced here: 98.2 us
  Pallas kernels  92.8 us (94%)
  local copies, waits for them, and re-layouts  4.78 us (5%)
    pallas_call x1, Pallas kernels, shards(): pl.pallas_call(kernel, out_shape=[jax.ShapeDtypeStruct((FINE_C, FINE), bf...  92.8 us
    unnamed x10, local copies, waits for them, and re-layouts  4.78 us

profile of v3, /device:TPU:1, one launch (start us, length us, event | category | flops | bytes accessed | tf_op | source)
XLA Modules:
  0.0 98.2 jit_solution(9052244535637461307)
XLA Ops:
  0.6 0.0 copy-start
  0.6 0.9 copy-done
  1.5 0.0 copy-start.1
  1.5 0.9 copy-done.1
  2.4 0.0 copy-start.2
  2.4 0.8 copy-done.2
  3.3 0.0 copy-start.3
  3.3 0.8 copy-done.3
  4.1 92.8 %shard_map.59 = (bf16[176,384]{1,0:T(8,128)(2,1)S(1)}, bf16[176,384]{1,0:T(8,128)(2,1)S(1)}) custom-call(bf16[176,384]{1,0:T(8,128)(2,1)S(1)} %bitcast.6, bf16[176,384]{1,0:T(8,128)(2,1)S(1)} %bitcast.7, bf16[5,24,176]{2,1,0:T(8,128)(2,1)S(1)} %bitcast.10, bf16[5,22,192]{2,1,0:T(8,128)(2,1)S(1)} %bitcast.11), custom_call_target="tpu_custom_call" | custom-call | tf_op jit(solution)/shard_map/pallas_call | solution.py:579
  96.9 0.7 copy.8
  97.5 0.7 copy.9
Async XLA Ops:
  0.6 0.9 copy-start
  1.5 0.9 copy-start.1
  2.4 0.8 copy-start.2
  3.3 0.8 copy-start.3

commit v4 on v3

--- a/solution.py
+++ b/solution.py
@@ -20,7 +20,7 @@
 POS, LANES, EDGE = 192, 256, 32
 FINE = 384
 WIDE = 128 + FINE + 128
-VMEM_LIMIT = 36 << 20
+VMEM_LIMIT = 56 << 20
 
 
 def erf(value):
@@ -69,14 +69,23 @@
 
 
 def kernel(
-    enc_ref, cot_ref, w1_ref, w2_ref, merged_ref, genc_ref,
+    enc_in, cot_in, w1_in, w2_in, merged_ref, genc_ref, w1_ref, w2_ref,
     edge_out, edge_in, enc_wide, cot_wide, w1_all, w1_swap, w2_all, w2_swap,
     pooled_own, pooled_other, x1, p1_send, p1_recv, pre_c, slope_c, c_own, c_other, x2,
     enc_rows, cot_rows, merged_rows, p2_send, p2_recv, g_send, g_recv, y1, y2, gc_out, gc_in,
     gc_send, gc_recv, y4, gp_out, gp_in,
-    halo_s, halo_r, near_s, near_r, first_s, first_r, second_s, second_r, swap_s, swap_r,
+    in_s, halo_s, halo_r, near_s, near_r, first_s, first_r, second_s, second_r, swap_s, swap_r,
     pair_s, pair_r, tp_s, tp_r,
 ):
+    own = slice(128, 128 + FINE)
+    loads = [
+        pltpu.make_async_copy(src, dst, in_s.at[n])
+        for n, (src, dst) in enumerate(
+            ((w1_in, w1_ref), (w2_in, w2_ref), (enc_in, enc_wide.at[:, own]), (cot_in, cot_wide.at[:, own]))
+        )
+    ]
+    for load in loads:
+        load.start()
     ctx, t = lax.axis_index("ctx"), lax.axis_index("tp")
     core = lax.rem(t, 2)
     mate = t + 1 - 2 * core
@@ -107,6 +116,8 @@
     for device in partners:
         pl.semaphore_signal(barrier, inc=1, device_id=device, device_id_type=MESH)
 
+    for load in loads:
+        load.wait()
     taps = ((w1_all, w1_swap), (w2_all, w2_swap))
     down = [w1_ref[k].astype(f32) for k in range(5)]
     up = [w2_ref[k].astype(f32) for k in range(5)]
@@ -115,12 +126,10 @@
     up = jnp.concatenate([up, jnp.zeros((ROWS - OUT2, L2), f32)], axis=0)
     for w_all, block in ((w1_all, down), (w2_all, up)):
         w_all[two, lax.div(one, 2), lax.rem(one, 2)] = block.astype(bf16)
-    enc_wide[:, 128 : 128 + FINE] = enc_ref[...]
-    cot_wide[:, 128 : 128 + FINE] = cot_ref[...]
     low = iota((FINE_C, 128), 1) < 64
-    last, first_tile = slice(FINE - 128, FINE), slice(0, 128)
-    enc_last, cot_last = enc_ref[:, last].astype(f32), shift(cot_ref[:, last].astype(f32), 64, 1)
-    enc_first, cot_first = enc_ref[:, first_tile].astype(f32), shift(cot_ref[:, first_tile].astype(f32), 64, 1)
+    last, first_tile = slice(FINE, 128 + FINE), slice(128, 256)
+    enc_last, cot_last = enc_wide[:, last].astype(f32), shift(cot_wide[:, last].astype(f32), 64, 1)
+    enc_first, cot_first = enc_wide[:, first_tile].astype(f32), shift(cot_wide[:, first_tile].astype(f32), 64, 1)
     edge_out[0] = jnp.where(low, cot_last, enc_last).astype(bf16)
     edge_out[1] = jnp.where(low, enc_first, cot_first).astype(bf16)
     pl.semaphore_wait(barrier, len(partners))
@@ -313,16 +322,16 @@
     def left(copy):
         copy.wait_send()
 
-    def with_taps(w, q, use):
-        w_all, w_swap = taps[w]
+    def own_taps(w, q, use):
+        w_all = taps[w][0]
 
         @pl.when(core == 0)
         def _():
-            use([flat(w_all[2 * n]) for n in q], [flat(w_swap[n]) for n in q])
+            use([flat(w_all[2 * n]) for n in q])
 
         @pl.when(core == 1)
         def _():
-            use([flat(w_all[:, n, 1]) for n in q], [flat(w_swap[n]) for n in q])
+            use([flat(w_all[:, n, 1]) for n in q])
 
     for d in (1, 7, 2, 6, 3, 5, 4):
         near(d).start()
@@ -389,11 +398,13 @@
 
         @pl.loop(2 * c, 2 * c + 2)
         def _(q):
-            def use(mine, swapped):
-                part = dot(mine[0], x1[0:L1]) + dot(swapped[0], x1[L1 : 2 * L1])
+            swapped = dot(flat(w1_swap[q]), x1[L1 : 2 * L1])
+
+            def use(mine):
+                part = dot(mine[0], x1[0:L1]) + swapped
                 p1_send[:, q] = part.reshape(RING, ROWS, LANES).astype(bf16)
 
-            with_taps(0, [q], use)
+            own_taps(0, [q], use)
 
         for d in order:
             scatter(0, c, p1_send, p1_recv, d).start()
@@ -495,22 +506,15 @@
 
     fine_grads(0, arrived, True)
     fine_grads(1, arrived, True)
-    for c in (0, 1):
-        columns = [lax.div(column(core, 2 * c + n), 2) for n in (0, 1)]
-        block = jnp.concatenate([flat(g_recv[:, 2 * c + n]) for n in (0, 1)], axis=0)
-
-        def add(mine, swapped):
-            for other, use in enumerate((mine, swapped)):
-                use = jnp.concatenate(use, axis=0)
-                sums = dot_first(block[:, 0:LANES], use[:, 0:640])
-                pairs = dot_first(block[:, LANES:], use[:, 640:1024])
-                if c == 0:
-                    y1[other], y2[other] = sums, pairs
-                else:
-                    y1[other] += sums
-                    y2[other] += pairs
-
-        with_taps(1, columns, add)
+    columns = [lax.div(column(core, slot), 2) for slot in range(4)]
+    block = jnp.concatenate([flat(g_recv[:, slot]) for slot in range(4)], axis=0)
+
+    def back_fine(other, use):
+        use = jnp.concatenate(use, axis=0)
+        y1[other] = dot_first(block[:, 0:LANES], use[:, 0:640])
+        y2[other] = dot_first(block[:, LANES:], use[:, 640:1024])
+
+    back_fine(1, [flat(w2_swap[n]) for n in columns])
 
     def coarse_part(other):
         total = shift(y1[other, :, 0:192] + y2[other, :, 0:192], -1, 0)
@@ -520,6 +524,7 @@
 
     gc_out[...] = coarse_part(1)
     pair(2, gc_out, gc_in).start()
+    own_taps(1, columns, lambda use: back_fine(0, use))
     own = coarse_part(0)
     pair(2, gc_out, gc_in).wait_recv()
     grad_c = jnp.where(inside, (own + gc_in[...]) * slope_c[...], 0.0).reshape(4, 2, ROWS, LANES).astype(bf16)
@@ -539,17 +544,19 @@
         for d in order:
             gather(6, c, gc_send, gc_recv, d).wait_recv()
 
-        block = jnp.concatenate([flat(gc_recv[:, 2 * c + n]) for n in (0, 1)], axis=0)
-
-        def add(mine, swapped):
-            for other, use in enumerate((mine, swapped)):
-                part = dot_first(block, jnp.concatenate(use, axis=0))
-                if c == 0:
-                    y4[other] = part
-                else:
-                    y4[other] += part
-
-        with_taps(0, [2 * c, 2 * c + 1], add)
+        coarse_block = jnp.concatenate([flat(gc_recv[:, 2 * c + n]) for n in (0, 1)], axis=0)
+        pair_of = [2 * c, 2 * c + 1]
+
+        def back_coarse(other, use, c=c, coarse_block=coarse_block):
+            part = dot_first(coarse_block, jnp.concatenate(use, axis=0))
+            if c == 0:
+                y4[other] = part
+            else:
+                y4[other] += part
+
+        back_coarse(1, [flat(w1_swap[n]) for n in pair_of])
+        if c == 0:
+            own_taps(0, pair_of, lambda use: back_coarse(0, use))
 
     def fine_part(other):
         total = None
@@ -560,6 +567,7 @@
 
     gp_out[...] = fine_part(1)
     pair(3, gp_out, gp_in).start()
+    own_taps(0, pair_of, lambda use: back_coarse(0, use))
     own = fine_part(0)
     for c in (0, 1):
         for d in order:
@@ -568,7 +576,7 @@
     total = (own + gp_in[...]) * 0.5
     high = total.astype(bf16)
     low = (total - high.astype(f32)).astype(bf16)
-    genc_ref[...] = (cot_ref[...].astype(f32) + dot(high, widen) + dot(low, widen)).astype(bf16)
+    genc_ref[...] = (cot_wide[:, 128 : 128 + FINE].astype(f32) + dot(high, widen) + dot(low, widen)).astype(bf16)
 
     pair(3, gp_out, gp_in).wait_send()
 
@@ -579,9 +587,11 @@
     merged, grad_enc = pl.pallas_call(
         kernel,
         out_shape=[jax.ShapeDtypeStruct((FINE_C, FINE), bf16)] * 2,
-        in_specs=[pl.BlockSpec(memory_space=vmem)] * 4,
+        in_specs=[pl.BlockSpec(memory_space=pltpu.HBM)] * 4,
         out_specs=[pl.BlockSpec(memory_space=vmem)] * 2,
         scratch_shapes=[
+            vmem((5, OUT1, FINE_C), bf16),
+            vmem((5, OUT2, COARSE_C), bf16),
             vmem((2, FINE_C, 128), bf16),
             vmem((2, FINE_C, 128), bf16),
             vmem((FINE_C, WIDE), bf16),
@@ -616,6 +626,7 @@
             vmem((2, LANES, L1), f32),
             vmem((FINE_C, LANES), f32),
             vmem((FINE_C, LANES), f32),
+            dma((4,)),
             dma((2,)),
             dma((2,)),
             dma((RING,)),

time: 98.4 us -> 95.3 us (0.968)
  local copies, waits for them, and re-layouts: 4.78 us -> 2.27 us
    unnamed x10 -> x4, local copies, waits for them, and re-layouts: 4.78 us -> 2.27 us
where the time goes in v4:
time: 95.3 us; the launch traced here: 95.2 us
  Pallas kernels  92.2 us (97%)
  local copies, waits for them, and re-layouts  2.27 us (2%)
    pallas_call x1, Pallas kernels, shards(): pl.pallas_call(kernel, out_shape=[jax.ShapeDtypeStruct((FINE_C, FINE), bf...  92.2 us
    unnamed x4, local copies, waits for them, and re-layouts  2.27 us

profile of v4, /device:TPU:1, one launch (start us, length us, event | category | flops | bytes accessed | tf_op | source)
XLA Modules:
  0.0 95.2 jit_solution(9763159392090680596)
XLA Ops:
  0.6 92.2 %shard_map.59 = (bf16[176,384]{1,0:T(8,128)(2,1)}, bf16[176,384]{1,0:T(8,128)(2,1)}) custom-call(bf16[176,384]{1,0:T(8,128)(2,1)} %bitcast.6, bf16[176,384]{1,0:T(8,128)(2,1)} %bitcast.7, bf16[5,24,176]{2,1,0:T(8,128)(2,1)} %bitcast.10, bf16[5,22,192]{2,1,0:T(8,128)(2,1)} %bitcast.11), custom_call_target="tpu_custom_call" | custom-call | tf_op jit(solution)/shard_map/pallas_call | solution.py:587
  92.9 0.0 copy-start
  92.9 1.6 %copy.8 = bf16[1,176,384]{2,1,0:T(8,128)(2,1)} copy(bf16[1,176,384]{2,1,0:T(8,128)(2,1)} %bitcast.9) | data formatting | bytes 270336
  94.5 0.0 copy-done
  94.5 0.7 copy.9
Async XLA Ops:
  92.9 1.6 %copy-start = (bf16[176,384]{1,0:T(8,128)(2,1)S(1)}, bf16[176,384]{1,0:T(8,128)(2,1)}, u32[]{:S(2)}) copy-start(bf16[176,384]{1,0:T(8,128)(2,1)} %get-tuple-element.5) | copy-start | bytes 405508

commit v5 on v4

--- a/solution.py
+++ b/solution.py
@@ -69,7 +69,7 @@
 
 
 def kernel(
-    enc_in, cot_in, w1_in, w2_in, merged_ref, genc_ref, w1_ref, w2_ref,
+    enc_in, cot_in, w1_in, w2_in, out_ref, w1_ref, w2_ref,
     edge_out, edge_in, enc_wide, cot_wide, w1_all, w1_swap, w2_all, w2_swap,
     pooled_own, pooled_other, x1, p1_send, p1_recv, pre_c, slope_c, c_own, c_other, x2,
     enc_rows, cot_rows, merged_rows, p2_send, p2_recv, g_send, g_recv, y1, y2, gc_out, gc_in,
@@ -438,13 +438,11 @@
         x2[other * L2 + 576 : other * L2 + 640] = jnp.zeros((64, 2 * LANES), bf16)
     second_step(1, 3)
     fine_swap_done(0)
-    for slot in range(3):
-        conv_fine([(slot, i) for i in rows_near])
+    conv_fine([(slot, i) for slot in range(3) for i in rows_near])
     fine_sums(0, begun)
     second_step(1, 4)
     fine_swap_done(1)
-    conv_fine([(slot, far) for slot in range(4)])
-    conv_fine([(3, i) for i in rows_near])
+    conv_fine([(slot, far) for slot in range(4)] + [(3, i) for i in rows_near])
     fine_sums(1, begun)
     p2_recv[t] = p2_send[t]
 
@@ -502,7 +500,7 @@
         iota((2 * LANES, FINE), 0) == lax.rem(back, 2) * LANES + lax.div(back, 2) + EDGE, 1.0, 0.0
     ).astype(bf16)
     kept = dot_first(spread, flat(merged_rows[...])).astype(bf16)
-    merged_ref[...] = dot(kept, unpick).astype(bf16)
+    out_ref[0] = dot(kept, unpick).astype(bf16)
 
     fine_grads(0, arrived, True)
     fine_grads(1, arrived, True)
@@ -576,7 +574,7 @@
     total = (own + gp_in[...]) * 0.5
     high = total.astype(bf16)
     low = (total - high.astype(f32)).astype(bf16)
-    genc_ref[...] = (cot_wide[:, 128 : 128 + FINE].astype(f32) + dot(high, widen) + dot(low, widen)).astype(bf16)
+    out_ref[1] = (cot_wide[:, 128 : 128 + FINE].astype(f32) + dot(high, widen) + dot(low, widen)).astype(bf16)
 
     pair(3, gp_out, gp_in).wait_send()
 
@@ -584,11 +582,11 @@
 def shards(enc, w_down, w_up, cot):
     dma = pltpu.SemaphoreType.DMA
     vmem = pltpu.VMEM
-    merged, grad_enc = pl.pallas_call(
+    both = pl.pallas_call(
         kernel,
-        out_shape=[jax.ShapeDtypeStruct((FINE_C, FINE), bf16)] * 2,
+        out_shape=jax.ShapeDtypeStruct((2, FINE_C, FINE), bf16),
         in_specs=[pl.BlockSpec(memory_space=pltpu.HBM)] * 4,
-        out_specs=[pl.BlockSpec(memory_space=vmem)] * 2,
+        out_specs=pl.BlockSpec(memory_space=vmem),
         scratch_shapes=[
             vmem((5, OUT1, FINE_C), bf16),
             vmem((5, OUT2, COARSE_C), bf16),
@@ -646,7 +644,7 @@
             collective_id=0, has_side_effects=True, vmem_limit_bytes=VMEM_LIMIT
         ),
     )(enc[0], cot[0], jnp.swapaxes(w_down, 1, 2), jnp.swapaxes(w_up, 1, 2))
-    return merged[None], grad_enc[None]
+    return both[0:1], both[1:2]
 
 
 def solution(mesh):

time: 95.3 us -> 94.8 us (level)
    unnamed x4 -> x0, local copies, waits for them, and re-layouts: 2.27 us -> none
    slice x0 -> x1, local copies, waits for them, and re-layouts: none -> 1.7 us  [shards(): return (both[0:1], both[1:2])]
where the time goes in v5:
time: 94.8 us; the launch traced here: 94.6 us
  Pallas kernels  92.3 us (97%)
  local copies, waits for them, and re-layouts  1.7 us (2%)
    pallas_call x1, Pallas kernels, shards(): pl.pallas_call(kernel, out_shape=jax.ShapeDtypeStruct((2, FINE_C, FINE),...  92.3 us

profile of v5, /device:TPU:1, one launch (start us, length us, event | category | flops | bytes accessed | tf_op | source)
XLA Modules:
  0.0 94.6 jit_solution(6074965375911426417)
XLA Ops:
  0.6 92.3 %shard_map.59 = bf16[2,176,384]{2,1,0:T(8,128)(2,1)} custom-call(bf16[176,384]{1,0:T(8,128)(2,1)} %bitcast.4, bf16[176,384]{1,0:T(8,128)(2,1)} %bitcast.5, bf16[5,24,176]{2,1,0:T(8,128)(2,1)} %bitcast.6, bf16[5,22,192]{2,1,0:T(8,128)(2,1)} %bitcast.7), custom_call_target="tpu_custom_call" | custom-call | tf_op jit(solution)/shard_map/pallas_call | solution.py:585
  92.9 1.7 %fusion = (bf16[1,176,384]{2,1,0:T(8,128)(2,1)}, bf16[1,176,384]{2,1,0:T(8,128)(2,1)}) fusion(bf16[2,176,384]{2,1,0:T(8,128)(2,1)} %shard_map.59), kind=kLoop, calls=%fused_computation | loop fusion | bytes 540672 | tf_op jit(solution)/shard_map/slice | solution.py:647

commit v6 on v5

--- a/solution.py
+++ b/solution.py
@@ -147,7 +147,8 @@
         block = w1_all.at[two, lax.div(j, 2), lax.rem(j, 2)]
         remote(block, block, near_s.at[d], near_r.at[d], (place(ring(one, d), two), t)).wait_recv()
 
-    routes = ((0, 1), (0, -1), (0, 2), (0, -2), (-2, 1), (-2, 2), (2, -1))
+    sign = 1 - 2 * lax.rem(one, 2)
+    routes = ((0, 1), (0, -1), (0, 2), (0, -2), (-2, 1), (-2 * sign, 2 * sign), (2, -1))
 
     def first(m, arriving=False):
         origin, step = routes[m]
@@ -372,6 +373,11 @@
     pooled_own[...] = pooled.astype(bf16)
     pair(0, pooled_own, pooled_other).start()
     second_step(0, 2)
+    for m in (0, 1, 4, 5, 6):
+        first(m, True).wait_recv()
+    for n in range(4):
+        second_start(1, n)
+    swap(1, two)
     enc_rows[...] = dot(spread, enc_ed.astype(bf16)).reshape(RING, ROWS, 2 * LANES).astype(bf16)
     cot_ed = dot(cot_wide[...], pick).astype(bf16)
     cot_rows[...] = dot(spread, cot_ed).reshape(RING, ROWS, 2 * LANES).astype(bf16)
@@ -382,17 +388,14 @@
             start = other * L1 + k * FINE_C
             x1[start : start + FINE_C] = shift(value, 2 - k, 1).astype(bf16)
         x1[other * L1 + 880 : (other + 1) * L1] = jnp.zeros((16, LANES), bf16)
-    for m in (0, 1, 4, 5, 6):
-        first(m, True).wait_recv()
     second_step(0, 3)
     for n in range(4):
-        second_start(1, n)
-    swap(1, two)
+        second_part(1, 1, n)
+    second_swap(1, 1)
     second_step(0, 4)
+    second_step(1, 2)
 
     for c in (0, 1):
-        second_part(1, 1, 2 * c)
-        second_part(1, 1, 2 * c + 1)
         if c == 0:
             swap_done(0)
 
@@ -410,8 +413,7 @@
             scatter(0, c, p1_send, p1_recv, d).start()
 
     p1_recv[t] = p1_send[t]
-    second_swap(1, 1)
-    second_step(1, 2)
+    second_step(1, 3)
     for c in (0, 1):
         for d in order:
             scatter(0, c, p1_send, p1_recv, d).wait_recv()
@@ -436,7 +438,6 @@
             x2[start : start + COARSE_C, 0:LANES] = even
             x2[start : start + COARSE_C, LANES : 2 * LANES] = odd
         x2[other * L2 + 576 : other * L2 + 640] = jnp.zeros((64, 2 * LANES), bf16)
-    second_step(1, 3)
     fine_swap_done(0)
     conv_fine([(slot, i) for slot in range(3) for i in rows_near])
     fine_sums(0, begun)

time: 94.8 us -> 94.5 us (level)
  no operation moved by 1% of the time
where the time goes in v6:
time: 94.5 us; the launch traced here: 94.4 us
  Pallas kernels  92 us (97%)
  local copies, waits for them, and re-layouts  1.7 us (2%)
    pallas_call x1, Pallas kernels, shards(): pl.pallas_call(kernel, out_shape=jax.ShapeDtypeStruct((2, FINE_C, FINE),...  92 us

profile of v6, /device:TPU:1, one launch (start us, length us, event | category | flops | bytes accessed | tf_op | source)
XLA Modules:
  0.0 94.4 jit_solution(7765844734507945057)
XLA Ops:
  0.6 92.0 %shard_map.59 = bf16[2,176,384]{2,1,0:T(8,128)(2,1)} custom-call(bf16[176,384]{1,0:T(8,128)(2,1)} %bitcast.4, bf16[176,384]{1,0:T(8,128)(2,1)} %bitcast.5, bf16[5,24,176]{2,1,0:T(8,128)(2,1)} %bitcast.6, bf16[5,22,192]{2,1,0:T(8,128)(2,1)} %bitcast.7), custom_call_target="tpu_custom_call" | custom-call | tf_op jit(solution)/shard_map/pallas_call | solution.py:586
  92.7 1.7 %fusion = (bf16[1,176,384]{2,1,0:T(8,128)(2,1)}, bf16[1,176,384]{2,1,0:T(8,128)(2,1)}) fusion(bf16[2,176,384]{2,1,0:T(8,128)(2,1)} %shard_map.59), kind=kLoop, calls=%fused_computation | loop fusion | bytes 540672 | tf_op jit(solution)/shard_map/slice | solution.py:648

commit v7 on v6

--- a/solution.py
+++ b/solution.py
@@ -249,7 +249,7 @@
         part = pl.ds(2 * c, 2)
         return to_group(n + c, d, send.at[lax.rem(lax.rem(t + d, GROUPS), 2), part], recv.at[t, part])
 
-    order = (4, 3, 5, 2, 6, 1, 7)
+    order = (4, 2, 6, 3, 5, 1, 7)
 
     far = ring(z, 4)
     rows_near = [ring(z, k) for k in range(-3, 4)]

time: 94.5 us -> 95 us (level)
  no operation moved by 1% of the time
where the time goes in v7:
time: 95 us; the launch traced here: 94.8 us
  Pallas kernels  92.5 us (97%)
  local copies, waits for them, and re-layouts  1.7 us (2%)
    pallas_call x1, Pallas kernels, shards(): pl.pallas_call(kernel, out_shape=jax.ShapeDtypeStruct((2, FINE_C, FINE),...  92.5 us

profile of v7, /device:TPU:1, one launch (start us, length us, event | category | flops | bytes accessed | tf_op | source)
XLA Modules:
  0.0 94.8 jit_solution(6168558907920218449)
XLA Ops:
  0.6 92.5 %shard_map.59 = bf16[2,176,384]{2,1,0:T(8,128)(2,1)} custom-call(bf16[176,384]{1,0:T(8,128)(2,1)} %bitcast.4, bf16[176,384]{1,0:T(8,128)(2,1)} %bitcast.5, bf16[5,24,176]{2,1,0:T(8,128)(2,1)} %bitcast.6, bf16[5,22,192]{2,1,0:T(8,128)(2,1)} %bitcast.7), custom_call_target="tpu_custom_call" | custom-call | tf_op jit(solution)/shard_map/pallas_call | solution.py:586
  93.1 1.7 %fusion = (bf16[1,176,384]{2,1,0:T(8,128)(2,1)}, bf16[1,176,384]{2,1,0:T(8,128)(2,1)}) fusion(bf16[2,176,384]{2,1,0:T(8,128)(2,1)} %shard_map.59), kind=kLoop, calls=%fused_computation | loop fusion | bytes 540672 | tf_op jit(solution)/shard_map/slice | solution.py:648
